TPU v7x, 256 devices: a whole 4x4x8 slice. The times are simulated.
256 devices in a mesh: tok: 4 (over z_lo), row: 8 (over y, z_hi), col: 8 (over x, core).
Axes of the slice: x: 4, y: 4, z: 8 (z_hi: 2, z_lo: 4; z = z_hi * 4 + z_lo), core: 2. Of those that a mesh axis runs over, the one named last changes fastest.
Arguments:
- tokens: bfloat16 [1024, 8192], P('tok', 'row'), may hold values from -6 to 6
- cotangent: bfloat16 [1024, 8192], P('tok', 'row'), may hold values from -6 to 6
- gate_weight: bfloat16 [8192, 16384], P('row', ('tok', 'col')), may hold values from -0.0625 to 0.0625
- up_weight: bfloat16 [8192, 16384], P('row', ('tok', 'col')), may hold values from -0.0625 to 0.0625
- down_weight: bfloat16 [16384, 8192], P(('tok', 'col'), 'row'), may hold values from -0.046875 to 0.046875
- gate_keep: int32 [512, 16384], P('row', ('tok', 'col')), may hold values from 0 to 65535
- up_keep: int32 [512, 16384], P('row', ('tok', 'col')), may hold values from 0 to 65535
- down_keep: int32 [1024, 8192], P(('tok', 'col'), 'row'), may hold values from 0 to 65535
Outputs:
- input_grad: bfloat16 [1024, 8192], P('tok', 'row')
- gate_grad: bfloat16 [8192, 16384], P('row', ('tok', 'col'))
- up_grad: bfloat16 [8192, 16384], P('row', ('tok', 'col'))
- down_grad: bfloat16 [16384, 8192], P(('tok', 'col'), 'row')
- gate_score: bfloat16 [8192, 16384], P('row', ('tok', 'col'))
- up_score: bfloat16 [8192, 16384], P('row', ('tok', 'col'))
- down_score: bfloat16 [16384, 8192], P(('tok', 'col'), 'row')
All inputs are finite; a program needn't handle non-finite values.
Results may differ from a plain program's by a relative error of at most 0.005.
Values may be sent and summed in bfloat16 or wider, within the bound.
A program may use at most 128 MiB of HBM per device.

v0:
```python
import jax
import jax.numpy as jnp
from jax import lax
from jax.sharding import PartitionSpec as P


def unpack_bits(packed):
    shifts = jnp.arange(16, dtype=jnp.int32)
    flags = jnp.right_shift(packed[:, None, :], shifts[None, :, None]) & 1
    return flags.reshape(packed.shape[0] * 16, packed.shape[1])


def activate(gate_pre, up_pre, back_pre):
    sigmoid_val = jax.nn.sigmoid(gate_pre)
    silu_value = gate_pre * sigmoid_val
    hidden = (silu_value * up_pre).astype(jnp.bfloat16)
    derivative = sigmoid_val * (1.0 + gate_pre * (1.0 - sigmoid_val))
    gate_back = (back_pre * up_pre * derivative).astype(jnp.bfloat16)
    up_back = (back_pre * silu_value).astype(jnp.bfloat16)
    return (hidden, gate_back, up_back)


def contract_rows(left, right):
    return lax.dot_general(
        left, right, (((0,), (0,)), ((), ())), preferred_element_type=jnp.float32
    )


def on_device(
    tokens, cotangent, gate_weight, up_weight, down_weight, gate_keep, up_keep, down_keep
):
    gate_mask = unpack_bits(gate_keep).astype(jnp.bfloat16)
    up_mask = unpack_bits(up_keep).astype(jnp.bfloat16)
    down_mask = unpack_bits(down_keep).astype(jnp.bfloat16)
    gate_eff = gate_weight * gate_mask
    up_eff = up_weight * up_mask
    down_eff = down_weight * down_mask
    tok_all, cot_all = (
        lax.all_gather(tokens, "tok", axis=0, tiled=True),
        lax.all_gather(cotangent, "tok", axis=0, tiled=True),
    )
    gate_part = jnp.dot(tok_all, gate_eff, preferred_element_type=jnp.float32)
    up_part = jnp.dot(tok_all, up_eff, preferred_element_type=jnp.float32)
    back_part = lax.dot_general(
        cot_all, down_eff, (((1,), (1,)), ((), ())), preferred_element_type=jnp.float32
    )
    gate_pre, up_pre, back_pre = lax.psum((gate_part, up_part, back_part), "row")
    hidden, gate_back, up_back = activate(gate_pre, up_pre, back_pre)
    down_full = contract_rows(hidden, cot_all)
    gate_full = contract_rows(tok_all, gate_back)
    up_full = contract_rows(tok_all, up_back)
    gate_grad = (gate_full * gate_mask.astype(jnp.float32)).astype(jnp.bfloat16)
    up_grad = (up_full * up_mask.astype(jnp.float32)).astype(jnp.bfloat16)
    down_grad = (down_full * down_mask.astype(jnp.float32)).astype(jnp.bfloat16)
    gate_score = (-(gate_weight.astype(jnp.float32) * gate_full)).astype(jnp.bfloat16)
    up_score = (-(up_weight.astype(jnp.float32) * up_full)).astype(jnp.bfloat16)
    down_score = (-(down_weight.astype(jnp.float32) * down_full)).astype(jnp.bfloat16)
    first = lax.dot_general(
        gate_back, gate_eff, (((1,), (1,)), ((), ())), preferred_element_type=jnp.float32
    )
    second = lax.dot_general(
        up_back, up_eff, (((1,), (1,)), ((), ())), preferred_element_type=jnp.float32
    )
    input_part = lax.psum_scatter(first + second, "tok", scatter_dimension=0, tiled=True)
    input_grad = lax.psum(input_part, "col").astype(jnp.bfloat16)
    return (input_grad, gate_grad, up_grad, down_grad, gate_score, up_score, down_score)


def solution(mesh):
    return jax.shard_map(
        on_device,
        mesh=mesh,
        in_specs=(
            P("tok", "row"),
            P("tok", "row"),
            P("row", ("tok", "col")),
            P("row", ("tok", "col")),
            P(("tok", "col"), "row"),
            P("row", ("tok", "col")),
            P("row", ("tok", "col")),
            P(("tok", "col"), "row"),
        ),
        out_specs=(
            P("tok", "row"),
            P("row", ("tok", "col")),
            P("row", ("tok", "col")),
            P(("tok", "col"), "row"),
            P("row", ("tok", "col")),
            P("row", ("tok", "col")),
            P(("tok", "col"), "row"),
        ),
        check_vma=False,
    )
```

profile of v0, /device:TPU:1, one launch (start us, length us, event | category | flops | bytes accessed | tf_op | source)
XLA Modules:
  0.0 780.4 jit_solution(15732288702511991782)
XLA Ops:
  7.2 0.0 copy-start.12
  7.2 0.0 all-gather.3.cloned.1.call-start
  7.2 0.7 all-gather.3.cloned.1.call-update
  7.9 0.0 all-gather.5.cloned.1.call-start
  8.0 0.7 all-gather.5.cloned.1.call-update
  8.7 0.0 all-reduce.4.cloned.1.call-start
  8.7 0.1 shift_right_arithmetic.63
  8.8 0.1 shift_right_arithmetic.69
  8.9 0.0 copy-start.14
  8.9 1.5 copy.26
  10.4 0.0 copy-done.12
  10.4 0.0 copy-start.3
  10.4 1.3 copy.28
  11.8 0.0 copy-done.14
  11.8 1.6 shift_right_arithmetic.72
  13.3 0.0 copy-start.15
  13.4 2.0 copy.27
  15.3 0.0 copy-done.15
  15.3 1.6 shift_right_arithmetic.66
  16.9 0.0 copy-start.13
  16.9 2.9 copy.25
  19.8 0.0 copy-done.13
  19.8 0.0 copy-start
  19.8 2.8 fusion.9
  22.6 0.0 copy-done
  22.6 0.0 copy-start.9
  22.6 1.3 and_convert_fusion.1
  23.9 0.0 copy-done.9
  23.9 1.4 fusion.14
  25.3 38.4 %all-gather.3.cloned.1.call-done = bf16[1024,1024]{1,0:T(8,128)(2,1)} async-done(((bf16[256,1024]{1,0:T(8,128)(2,1)}), bf16[1024,1024]{1,0:T(8,128)(2,1)}) %all-gather.3.cloned.1.call-update) | async-done | bytes 2097168 | tf_op jit(solution)/shard_map/all_gather | solution.py:40
  63.7 4.5 convolution_bitcast_fusion.2
  68.2 47.1 %all-gather.5.cloned.1.call-done = bf16[1024,1024]{1,0:T(8,128)(2,1)} async-done(((bf16[256,1024]{1,0:T(8,128)(2,1)}), bf16[1024,1024]{1,0:T(8,128)(2,1)}) %all-gather.5.cloned.1.call-update) | async-done | bytes 2097168 | tf_op jit(solution)/shard_map/all_gather | solution.py:39
  115.3 4.6 convolution_bitcast_fusion
  120.0 0.0 copy-done.3
  120.0 0.0 copy-done.6
  120.0 0.0 copy-done.16
  120.0 2.6 convolution_bitcast_fusion.1
  122.6 0.0 all-reduce.4.cloned.1.call-update
  122.6 0.2 reduce-scatter.2.cloned.1.call-start
  122.8 512.4 %all-reduce.4.cloned.1.call-done = (f32[1024,512]{0,1:T(8,128)}, f32[1024,512]{0,1:T(8,128)}, f32[1024,512]{0,1:T(8,128)}) async-done(((f32[1024,512]{0,1:T(8,128)}, f32[1024,512]{0,1:T(8,128)}, f32[1024,512]{0,1:T(8,128)}), (f32[1024,512]{0,1:T(8,128)}, f32[1024,512]{0,1:T(8,128)}, f32[1024,512]{0,1:T(8,128)})) %all-reduce.4.cloned.1.call-update) | async-done | bytes 6291472 | tf_op jit(solution)/shard_map/psum | solution.py:47
  635.3 4.2 multiply_convert_fusion.2
  639.5 0.0 copy-start.2
  639.5 0.0 copy-done.10
  639.5 0.0 copy-start.4
  639.5 0.0 copy-start.7
  639.5 1.3 fusion.16
  640.8 0.0 copy-done.2
  640.8 0.3 copy-done.4
  641.1 0.3 copy-done.7
  641.4 3.3 convolution_add_fusion
  644.7 0.0 reduce-scatter.2.cloned.1.call-update
  644.7 5.0 fusion.5
  649.7 2.4 copy.33
  652.1 0.0 copy-done.5
  652.1 0.0 copy-done.8
  652.1 4.8 fusion.2
  656.9 2.3 copy.34
  659.2 2.4 copy.32
  661.6 2.3 copy.31
  663.9 0.0 copy-done.1
  663.9 0.0 copy-done.11
  663.9 5.1 negate_convert_fusion
  669.0 53.7 %reduce-scatter.2.cloned.1.call-done = f32[256,1024]{1,0:T(8,128)} async-done(((f32[1024,1024]{1,0:T(8,128)}), f32[256,1024]{1,0:T(8,128)}) %reduce-scatter.2.cloned.1.call-update) | async-done | bytes 1048592 | tf_op jit(solution)/shard_map/reduce_scatter | solution.py:64
  722.7 51.1 %all-reduce.5 = bf16[256,1024]{1,0:T(8,128)(2,1)} all-reduce(f32[256,1024]{1,0:T(8,128)} %reduce-scatter.2.cloned.1.call-done), channel_id=1, replica_groups=mesh['tok'=4,'row'=8,'col'=8] {'col'}, use_global_device_ids=true, to_apply=%region_4.0 | all-reduce | flops 262144 | bytes 1572864 | tf_op jit(solution)/shard_map/psum | solution.py:65
  (9 shorter events, 0.0 us)
Async XLA Ops:
  7.2 3.2 copy-start.12
  7.2 56.5 %all-gather.3.cloned.1.call-start = ((), (), s32[]{:S(2)}) async-start(), calls=%async_computation.1 | async-start | bytes 2621440 | tf_op jit(solution)/shard_map/all_gather | solution.py:40
  7.9 107.4 %all-gather.5.cloned.1.call-start = ((), (), s32[]{:S(2)}) async-start(), calls=%async_computation.2 | async-start | bytes 2621440 | tf_op jit(solution)/shard_map/all_gather | solution.py:39
  8.7 626.6 %all-reduce.4.cloned.1.call-start = ((), (), s32[]{:S(2)}) async-start(), calls=%async_computation.4 | async-start | bytes 12582912 | tf_op jit(solution)/shard_map/psum | solution.py:47
  8.9 2.9 copy-start.14
  10.4 109.6 %copy-start.3 = (bf16[1024,512]{0,1:T(8,128)(2,1)}, bf16[1024,512]{0,1:T(8,128)(2,1)S(1)}, u32[]{:S(2)}) copy-start(bf16[1024,512]{0,1:T(8,128)(2,1)S(1)} %copy.26) | copy-start | bytes 3145732
  13.3 2.0 copy-start.15
  16.9 2.9 copy-start.13
  19.8 2.8 copy-start
  22.6 1.3 copy-start.9
  115.3 4.6 copy-start.6
  115.3 4.6 copy-start.16
  122.6 600.1 %reduce-scatter.2.cloned.1.call-start = ((), (), s32[]{:S(2)}) async-start(), calls=%async_computation.3 | async-start | bytes 5242880 | tf_op jit(solution)/shard_map/reduce_scatter | solution.py:64
  635.3 4.2 copy-start.10
  639.5 1.3 copy-start.2
  639.5 1.6 copy-start.4
  639.5 1.9 copy-start.7
  649.7 2.4 copy-start.5
  649.7 2.4 copy-start.8
  659.2 4.7 copy-start.1
  659.2 4.7 copy-start.11
Sparse Core Ops, SparseCore 0:
  9.8 53.8 all-gather.2
  65.5 49.7 all-gather.4
  122.7 512.4 all-reduce.3
  644.9 77.8 reduce-scatter.1
where the time goes:
time: 782 us; the launch traced here: 780 us
  waiting for transfers between devices  653 us (84%)
  blocking collectives  51.1 us (7%)
  matrix products  31.2 us (4%)
  local copies, waits for them, and re-layouts  21.1 us (3%)
  between operations  13.9 us (2%)
  other arithmetic  9.66 us (1%)
    psum x1, waiting for transfers between devices, on_device(): lax.psum((gate_part, up_part, back_part), 'row')  512 us
    reduce_scatter x1, waiting for transfers between devices, on_device(): lax.psum_scatter(first + second, 'tok', scatter_dimension=0, tiled=True)  53.7 us
    psum x1, blocking collectives, on_device(): input_grad = lax.psum(input_part, 'col').astype(jnp.bfloat16)  51.1 us
    all_gather x1, waiting for transfers between devices, on_device(): lax.all_gather(tokens, 'tok', axis=0, tiled=True)  47.1 us
    all_gather x1, waiting for transfers between devices, on_device(): lax.all_gather(cotangent, 'tok', axis=0, tiled=True)  38.4 us
  transfers between devices with their start and end apart: 4, of which 4 were waited for; matrix products, arithmetic and copies ran while one was open for 6% of the time, Pallas kernels for 0%

commit v1 on v0

v1 whole, which is shorter than its diff:
```python
import functools

import jax
import jax.numpy as jnp
from jax import lax
from jax.experimental import pallas as pl
from jax.experimental.pallas import tpu as pltpu
from jax.sharding import PartitionSpec as P

MESH = pl.DeviceIdType.MESH
BF = jnp.bfloat16
F32 = jnp.float32
NCH = 8
T = 128
H = 16
LAG = dict(ax=-2, ac=-1, s1=0, s2=0, s3=1, s4=2, s5=3, s6=4, s7=5, s8=6)
ORDER = ("ax", "ac", "s1", "s2", "s3", "s4", "s5", "s6", "s7", "s8")


def apply_mask(w_ref, keep_ref):
    cols = w_ref.shape[1]
    shifts = lax.broadcasted_iota(jnp.int32, (16, cols), 0)

    def one(i, _):
        row = jnp.broadcast_to(keep_ref[pl.ds(i, 1), :], (16, cols))
        bits = (jnp.right_shift(row, shifts) & 1).astype(F32)
        at = pl.ds(pl.multiple_of(i * 16, 16), 16)
        w_ref[at, :] = (w_ref[at, :].astype(F32) * bits).astype(BF)
        return 0

    lax.fori_loop(0, keep_ref.shape[0], one, 0, unroll=4)


def comm_kernel(
    tokens, cot, gate_w, up_w, down_w, gate_k, up_k, down_k,
    out, tc_out, g_out,
    tc, gw, uw, dw, gk, uk, dk, pre, pre32, rx1, acc, rx3, hs, hr, keep, act,
    dpart, d32, dr, zown, zs, zr, obuf,
    ld_sem, send_sem, az, ax, ac, s1, s3, hrs, gh, gy, drs, zrs, ors, st_sem,
):
    t = lax.axis_index("tok")
    r = lax.axis_index("row")
    c = lax.axis_index("col")
    y, h = r // 2, r % 2
    x, k = c // 2, c % 2
    y_next, y_prev, y_opp = (y + 1) % 4, (y + 3) % 4, (y + 2) % 4
    at_next, at_prev = (t, y_next * 2 + h, c), (t, y_prev * 2 + h, c)
    at_twin = (t, y * 2 + (1 - h), c)
    at_core = (t, r, x * 2 + (1 - k))

    def tok_xor(n):
        return (t % 2 + n % 2) % 2 + 2 * ((t // 2 + n // 2) % 2)

    mine = pl.ds(pl.multiple_of(t * 256, 256), 256)
    loads = [
        pltpu.make_async_copy(src, dst, ld_sem.at[n])
        for n, (src, dst) in enumerate(
            (
                (tokens, tc.at[0, mine]), (cot, tc.at[1, mine]),
                (gate_k, gk), (gate_w, gw), (up_k, uk), (up_w, uw),
                (down_k, dk), (down_w, dw),
            )
        )
    ]
    for copy in loads:
        copy.start()

    barrier = pltpu.get_barrier_semaphore()
    peers = [at_next, at_prev, at_twin]
    peers += [(t, r, (c + n) % 8) for n in range(1, 8)]
    peers += [(tok_xor(n), r, c) for n in range(1, 4)]
    for peer in peers:
        pl.semaphore_signal(barrier, inc=1, device_id=peer, device_id_type=MESH)

    SEND = dict(az=0, ax=1, ac=2, rs=3, ag=4, d=5, z=6, o=7)

    def send(src, dst, cls, recv, peer):
        pltpu.make_async_remote_copy(
            src_ref=src, dst_ref=dst, send_sem=send_sem.at[SEND[cls]], recv_sem=recv,
            device_id=peer, device_id_type=MESH,
        ).start()

    def wait(ref, sem):
        pltpu.make_async_copy(ref, ref, sem).wait()

    def base(i):
        return tok_xor(i // 2) * 256 + (i % 2) * T

    def rows(i, q, n=H):
        return pl.ds(pl.multiple_of(base(i) + q * n, n), n)

    def stage_az(i):
        at = pl.ds(pl.multiple_of(t * 256 + (i % 2) * T + x * 32, 32), 32)
        send(tc.at[k, at], tc.at[k, at], "az", az.at[i], (tok_xor(i // 2), r, c))

    def stage_ax(i):
        if i < 2:
            return
        at = rows(i, x, 32)
        wait(tc.at[k, at], az.at[i])
        for n in (1, 3, 2):
            send(tc.at[k, at], tc.at[k, at], "ax", ax.at[i], (t, r, ((x + n) % 4) * 2 + k))

    def stage_ac(i):
        if i < 2:
            return
        wait(tc.at[k, pl.ds(0, 96)], ax.at[i])
        at = rows(i, 0, T)
        send(tc.at[k, at], tc.at[k, at], "ac", ac.at[i], at_core)

    def stage_s1(i):
        at = rows(i, 0, T)
        if i >= 2:
            wait(tc.at[1 - k, at], ac.at[i])
        tok_rows = tc[0, at, :]
        cot_rows = tc[1, at, :]
        parts = (
            jnp.dot(tok_rows, gw[...], preferred_element_type=F32),
            jnp.dot(tok_rows, uw[...], preferred_element_type=F32),
            lax.dot_general(
                cot_rows, dw[...], (((1,), (1,)), ((), ())), preferred_element_type=F32
            ),
        )
        for n, part in enumerate(parts):
            pre32[at, pl.ds(n * 512, 512)] = part
            pre[at, pl.ds(n * 512, 512)] = part.astype(BF)
        send(pre.at[rows(i, y_opp * 2)], rx1.at[i, 0], "rs", s1.at[i], at_next)
        send(pre.at[rows(i, y_opp * 2 + 1)], rx1.at[i, 1], "rs", s1.at[i], at_prev)
        send(pre.at[rows(i, y_next * 2 + 1)], rx3.at[i, 0], "rs", s3.at[i], at_next)
        send(pre.at[rows(i, y_prev * 2)], rx3.at[i, 1], "rs", s3.at[i], at_prev)

    def stage_s2(i):
        wait(rx1.at[i], s1.at[i])
        acc[i, 0] = (rx1[i, 0].astype(F32) + pre32[rows(i, y_next * 2), :]).astype(BF)
        send(acc.at[i, 0], rx3.at[i, 2], "rs", s3.at[i], at_next)
        acc[i, 1] = (rx1[i, 1].astype(F32) + pre32[rows(i, y_prev * 2 + 1), :]).astype(BF)
        send(acc.at[i, 1], rx3.at[i, 3], "rs", s3.at[i], at_prev)

    def stage_s3(i):
        wait(rx3.at[i], s3.at[i])

        def total(half):
            return (
                pre32[rows(i, y * 2 + half), :]
                + rx3[i, 1 - half].astype(F32)
                + rx3[i, 2 + half].astype(F32)
            )

        hs[i] = total(1 - h).astype(BF)
        send(hs.at[i], hr.at[i], "rs", hrs.at[i], at_twin)
        keep[i] = total(h)

    def stage_s4(i):
        wait(hr.at[i], hrs.at[i])
        sums = keep[i] + hr[i].astype(F32)
        gate, up, back = sums[:, :512], sums[:, 512:1024], sums[:, 1024:]
        sig = jax.nn.sigmoid(gate)
        silu = gate * sig
        at = rows(i, r)
        act[at, pl.ds(0, 512)] = (silu * up).astype(BF)
        act[at, pl.ds(512, 512)] = (back * up * (sig * (1.0 + gate * (1.0 - sig)))).astype(BF)
        act[at, pl.ds(1024, 512)] = (back * silu).astype(BF)
        send(act.at[at], act.at[at], "ag", gh.at[i], at_twin)
        send(act.at[at], act.at[at], "ag", gy.at[i, h], at_next)
        send(act.at[at], act.at[at], "ag", gy.at[i, 1 - h], at_prev)

    def stage_s5(i):
        at = rows(i, y * 2 + (1 - h))
        wait(act.at[at], gh.at[i])
        send(act.at[at], act.at[at], "ag", gy.at[i, 1 - h], at_next)
        send(act.at[at], act.at[at], "ag", gy.at[i, h], at_prev)

    def stage_s6(i):
        wait(act.at[pl.ds(0, 2 * H)], gy.at[i, 0])
        at = rows(i, y_prev * 2)
        send(act.at[at], act.at[at], "ag", gy.at[i, 1], at_next)
        at = rows(i, y_next * 2 + 1)
        send(act.at[at], act.at[at], "ag", gy.at[i, 1], at_prev)

    def stage_s7(i):
        wait(act.at[pl.ds(0, 4 * H)], gy.at[i, 1])
        at = rows(i, 0, T)
        nt = (((1,), (1,)), ((), ()))
        part = lax.dot_general(
            act[at, pl.ds(512, 512)], gw[...], nt, preferred_element_type=F32
        ) + lax.dot_general(
            act[at, pl.ds(1024, 512)], uw[...], nt, preferred_element_type=F32
        )
        d32[i] = part
        dpart[at, :] = part.astype(BF)
        for n in range(7):
            peer = (c + n + 1) % 8
            send(dpart.at[rows(i, peer)], dr.at[i, n], "d", drs.at[i], (t, r, peer))

    def stage_s8(i):
        wait(dr.at[i], drs.at[i])
        total = d32[i, pl.ds(pl.multiple_of(c * H, H), H), :]
        for n in range(7):
            total = total + dr[i, n].astype(F32)
        if i < 2:
            zown[i] = total
        else:
            zs[i - 2] = total
            send(zs.at[i - 2], zr.at[i - 2], "z", zrs.at[i - 2], (tok_xor(i // 2), r, c))

    def stage_s9(u):
        total = zown[u]
        for n in range(3):
            wait(zr.at[2 * n + u], zrs.at[2 * n + u])
            total = total + zr[2 * n + u]
        at = pl.ds(pl.multiple_of(u * T + c * H, H), H)
        obuf[at, :] = total.astype(BF)
        for n in range(7):
            send(obuf.at[at], obuf.at[at], "o", ors.at[u], (t, r, (c + n + 1) % 8))

    loads[0].wait()
    loads[1].wait()
    pl.semaphore_wait(barrier, len(peers))
    for i in range(2, NCH):
        stage_az(i)
    for n, (w, kk) in enumerate(((gw, gk), (uw, uk), (dw, dk))):
        loads[2 + 2 * n].wait()
        loads[3 + 2 * n].wait()
        apply_mask(w, kk)

    stages = dict(
        ax=stage_ax, ac=stage_ac, s1=stage_s1, s2=stage_s2, s3=stage_s3, s4=stage_s4,
        s5=stage_s5, s6=stage_s6, s7=stage_s7, s8=stage_s8,
    )
    for tick in range(min(LAG.values()), NCH + max(LAG.values())):
        for name in ORDER:
            i = tick - LAG[name]
            if 0 <= i < NCH:
                stages[name](i)
                if name == "s7" and i == NCH - 1:
                    stores = [
                        pltpu.make_async_copy(tc, tc_out, st_sem.at[0]),
                        pltpu.make_async_copy(act, g_out, st_sem.at[1]),
                    ]
                    for copy in stores:
                        copy.start()
                if name == "s8" and i >= NCH - 2:
                    stage_s9(i - (NCH - 2))
    for u in range(2):
        wait(obuf.at[pl.ds(0, 7 * H)], ors.at[u])
    last = pltpu.make_async_copy(obuf, out, st_sem.at[2])
    last.start()
    for copy in stores + [last]:
        copy.wait()
    wait(tc.at[0, pl.ds(0, 6 * 32)], send_sem.at[0])
    wait(tc.at[0, pl.ds(0, 18 * 32)], send_sem.at[1])
    wait(tc.at[0, pl.ds(0, 6 * T)], send_sem.at[2])
    wait(pre.at[pl.ds(0, 56 * H)], send_sem.at[3])
    wait(act.at[pl.ds(0, 56 * H)], send_sem.at[4])
    wait(dpart.at[pl.ds(0, 56 * H)], send_sem.at[5])
    wait(zs, send_sem.at[6])
    wait(obuf.at[pl.ds(0, 14 * H)], send_sem.at[7])


def grad_kernel(
    tok, cot, hidden, gate_back, up_back, gate_w, up_w, down_w, gate_k, up_k, down_k,
    gate_g, up_g, down_g, gate_s, up_s, down_s,
):
    def finish(full, w_ref, keep_ref, g_ref, s_ref):
        n, cols = keep_ref.shape
        shifts = lax.broadcasted_iota(jnp.int32, (16, cols), 0)
        s_ref[...] = (-(w_ref[...].astype(F32) * full)).astype(BF)
        for i in range(n):
            row = jnp.broadcast_to(keep_ref[i : i + 1, :], (16, cols))
            bits = (jnp.right_shift(row, shifts) & 1).astype(F32)
            g_ref[16 * i : 16 * i + 16, :] = (full[16 * i : 16 * i + 16, :] * bits).astype(BF)

    tn = (((0,), (0,)), ((), ()))
    left = tok[0]
    full = lax.dot_general(left, gate_back[...], tn, preferred_element_type=F32)
    finish(full, gate_w, gate_k, gate_g, gate_s)
    full = lax.dot_general(left, up_back[...], tn, preferred_element_type=F32)
    finish(full, up_w, up_k, up_g, up_s)
    full = lax.dot_general(hidden[...], cot[0], tn, preferred_element_type=F32)
    finish(full, down_w, down_k, down_g, down_s)


def on_device(tokens, cot, gate_w, up_w, down_w, gate_k, up_k, down_k):
    any_spec = pl.BlockSpec(memory_space=pltpu.HBM)
    dma = pltpu.SemaphoreType.DMA
    out, tc, act = pl.pallas_call(
        comm_kernel,
        name="exchange",
        out_shape=(
            jax.ShapeDtypeStruct((256, 1024), BF),
            jax.ShapeDtypeStruct((2, 1024, 1024), BF),
            jax.ShapeDtypeStruct((1024, 1536), BF),
        ),
        in_specs=[any_spec] * 8,
        out_specs=(any_spec,) * 3,
        scratch_shapes=[
            pltpu.VMEM((2, 1024, 1024), BF),
            pltpu.VMEM((1024, 512), BF),
            pltpu.VMEM((1024, 512), BF),
            pltpu.VMEM((512, 1024), BF),
            pltpu.VMEM((64, 512), jnp.int32),
            pltpu.VMEM((64, 512), jnp.int32),
            pltpu.VMEM((32, 1024), jnp.int32),
            pltpu.VMEM((1024, 1536), BF),
            pltpu.VMEM((1024, 1536), F32),
            pltpu.VMEM((NCH, 2, H, 1536), BF),
            pltpu.VMEM((NCH, 2, H, 1536), BF),
            pltpu.VMEM((NCH, 4, H, 1536), BF),
            pltpu.VMEM((NCH, H, 1536), BF),
            pltpu.VMEM((NCH, H, 1536), BF),
            pltpu.VMEM((NCH, H, 1536), F32),
            pltpu.VMEM((1024, 1536), BF),
            pltpu.VMEM((1024, 1024), BF),
            pltpu.VMEM((NCH, T, 1024), F32),
            pltpu.VMEM((NCH, 7, H, 1024), BF),
            pltpu.VMEM((2, H, 1024), F32),
            pltpu.VMEM((6, H, 1024), F32),
            pltpu.VMEM((6, H, 1024), F32),
            pltpu.VMEM((256, 1024), BF),
            dma((8,)),
            dma((8,)),
            dma((NCH,)),
            dma((NCH,)),
            dma((NCH,)),
            dma((NCH,)),
            dma((NCH,)),
            dma((NCH,)),
            dma((NCH,)),
            dma((NCH, 2)),
            dma((NCH,)),
            dma((6,)),
            dma((2,)),
            dma((3,)),
        ],
        compiler_params=pltpu.CompilerParams(
            collective_id=0, has_side_effects=True, vmem_limit_bytes=48 * 2**20
        ),
    )(tokens, cot, gate_w, up_w, down_w, gate_k, up_k, down_k)

    n = 4
    wide = pl.BlockSpec((1024 // n, 512), lambda i: (i, 0))
    tall = pl.BlockSpec((512 // n, 1024), lambda i: (i, 0))
    wide_keep = pl.BlockSpec((64 // n, 512), lambda i: (i, 0))
    tall_keep = pl.BlockSpec((32 // n, 1024), lambda i: (i, 0))
    up_shape = jax.ShapeDtypeStruct((1024, 512), BF)
    down_shape = jax.ShapeDtypeStruct((512, 1024), BF)
    grads = pl.pallas_call(
        grad_kernel,
        name="weight_grads",
        grid=(n,),
        out_shape=(up_shape, up_shape, down_shape) * 2,
        in_specs=[
            pl.BlockSpec((1, 1024, 1024 // n), lambda i: (0, 0, i)),
            pl.BlockSpec((1, 1024, 1024), lambda i: (1, 0, 0)),
            pl.BlockSpec((1024, 512 // n), lambda i: (0, i)),
            pl.BlockSpec((1024, 512), lambda i: (0, 1)),
            pl.BlockSpec((1024, 512), lambda i: (0, 2)),
            wide, wide, tall, wide_keep, wide_keep, tall_keep,
        ],
        out_specs=(wide, wide, tall) * 2,
        compiler_params=pltpu.CompilerParams(vmem_limit_bytes=48 * 2**20),
    )(tc, tc, act, act, act, gate_w, up_w, down_w, gate_k, up_k, down_k)
    return (out, *grads)


def solution(mesh):
    return jax.shard_map(
        on_device,
        mesh=mesh,
        in_specs=(
            P("tok", "row"),
            P("tok", "row"),
            P("row", ("tok", "col")),
            P("row", ("tok", "col")),
            P(("tok", "col"), "row"),
            P("row", ("tok", "col")),
            P("row", ("tok", "col")),
            P(("tok", "col"), "row"),
        ),
        out_specs=(
            P("tok", "row"),
            P("row", ("tok", "col")),
            P("row", ("tok", "col")),
            P(("tok", "col"), "row"),
            P("row", ("tok", "col")),
            P("row", ("tok", "col")),
            P(("tok", "col"), "row"),
        ),
        check_vma=False,
    )
```

time: 782 us -> 128 us (0.16)
  waiting for transfers between devices: 653 us -> 0 us
  Pallas kernels: 0 us -> 118 us
  blocking collectives: 51.1 us -> 0 us
  matrix products: 31.2 us -> 0 us
  between operations: 13.9 us -> 0.68 us
  local copies, waits for them, and re-layouts: 21.1 us -> 9.26 us
  other arithmetic: 9.66 us -> 0 us
    psum x1 -> x0, waiting for transfers between devices: 512 us -> none  [on_device(): lax.psum((gate_part, up_part, back_part), 'row')]
    pallas_call x0 -> x2, Pallas kernels: none -> 118 us  [the longest x1 109 us: on_device(): pl.pallas_call(comm_kernel, name='exchange', out_shape=(jax.ShapeDtypeStr...]
    all_gather x2 -> x0, waiting for transfers between devices: 85.5 us -> none  [the longest x1 47.1 us: on_device(): lax.all_gather(tokens, 'tok', axis=0, tiled=True)]
    reduce_scatter x1 -> x0, waiting for transfers between devices: 53.7 us -> none  [on_device(): lax.psum_scatter(first + second, 'tok', scatter_dimension=0, tiled=True)]
    psum x1 -> x0, blocking collectives: 51.1 us -> none  [on_device(): input_grad = lax.psum(input_part, 'col').astype(jnp.bfloat16)]
    dot_general x8 -> x0, matrix products: 31.2 us -> none  [the longest x3 14.9 us: contract_rows(): lax.dot_general(left, right, (((0,), (0,)), ((), ())), preferred_element_...]
    shift_right_arithmetic x8 -> x0, local copies, waits for them, and re-layouts: 8.21 us -> none  [unpack_bits(): flags = jnp.right_shift(packed[:, None, :], shifts[None, :, None]) & 1]
  transfers between devices with their start and end apart: 4 -> 0, of which waited for: 4 -> 0; matrix products, arithmetic and copies ran while one was open for 6% -> 0% of each run, Pallas kernels for 0% -> 0%
where the time goes in v1:
time: 128 us; the launch traced here: 127 us
  Pallas kernels  118 us (92%)
  local copies, waits for them, and re-layouts  9.26 us (7%)
    pallas_call x1, Pallas kernels, on_device(): pl.pallas_call(comm_kernel, name='exchange', out_shape=(jax.ShapeDtypeStr...  109 us
    unnamed x23, local copies, waits for them, and re-layouts  9.26 us
    pallas_call x1, Pallas kernels, on_device(): pl.pallas_call(grad_kernel, name='weight_grads', grid=(n,), out_shape=(up...  8.42 us

profile of v1, /device:TPU:1, one launch (start us, length us, event | category | flops | bytes accessed | tf_op | source)
XLA Modules:
  0.0 127.5 jit_solution(8143616398546796146)
XLA Ops:
  0.6 0.0 copy-start
  0.6 1.2 copy-done
  1.9 0.0 copy-start.2
  1.9 1.2 copy-done.2
  3.1 0.0 copy-start.4
  3.1 1.2 copy-done.4
  4.3 0.0 copy-start.6
  4.3 0.9 copy-done.6
  5.2 0.0 copy-start.7
  5.2 0.9 copy-done.7
  6.1 0.0 copy-start.8
  6.1 0.9 copy-done.8
  7.0 0.0 copy-start.9
  7.0 1.0 copy-done.9
  8.1 0.0 copy-start.10
  8.1 1.0 copy-done.10
  9.1 0.0 copy-start.1
  9.1 0.0 copy-start.3
  9.1 0.0 copy-start.5
  9.1 109.1 %exchange.1 = (bf16[256,1024]{1,0:T(8,128)(2,1)S(1)}, bf16[2,1024,1024]{2,1,0:T(8,128)(2,1)}, bf16[1024,1536]{1,0:T(8,128)(2,1)}) custom-call(bf16[256,1024]{1,0:T(8,128)(2,1)S(1)} %copy-done.9, bf16[256,1024]{1,0:T(8,128)(2,1)S(1)} %copy-done.10, bf16[1024,512]{1,0:T(8,128)(2,1)S(1)} %copy-done, bf16[1024,512]{1,0:T(8,128)(2,1)S(1)} %copy-done.2, ...), custom_call_target="tpu_custom_call" | custom-call | tf_op jit(solution)/shard_map/exchange/pallas_call | solution.py:286
  118.3 0.0 copy-done.1
  118.3 0.0 copy-done.3
  118.3 0.0 copy-done.5
  118.3 8.4 %weight_grads.1 = (bf16[1024,512]{1,0:T(8,128)(2,1)}, bf16[1024,512]{1,0:T(8,128)(2,1)}, bf16[512,1024]{1,0:T(8,128)(2,1)}, bf16[1024,512]{1,0:T(8,128)(2,1)}, b...) custom-call(bf16[2,1024,1024]{2,1,0:T(8,128)(2,1)} %get-tuple-element.17.tok.cot, ...), custom_call_target="tpu_custom_call" | custom-call | tf_op jit(solution)/shard_map/weight_grads/pallas_call | solution.py:347
  126.7 0.8 copy.16
Async XLA Ops:
  0.6 1.2 copy-start
  1.9 1.2 copy-start.2
  3.1 1.2 copy-start.4
  4.3 0.9 copy-start.6
  5.2 0.9 copy-start.7
  6.1 0.9 copy-start.8
  7.0 1.0 copy-start.9
  8.1 1.0 copy-start.10
  9.1 109.1 %copy-start.1 = (bf16[1024,512]{1,0:T(8,128)(2,1)S(1)}, bf16[1024,512]{1,0:T(8,128)(2,1)}, u32[]{:S(2)}) copy-start(bf16[1024,512]{1,0:T(8,128)(2,1)} %gate_w.3) | copy-start | bytes 3145732
  9.1 109.2 %copy-start.3 = (bf16[1024,512]{1,0:T(8,128)(2,1)S(1)}, bf16[1024,512]{1,0:T(8,128)(2,1)}, u32[]{:S(2)}) copy-start(bf16[1024,512]{1,0:T(8,128)(2,1)} %up_w.3) | copy-start | bytes 3145732
  9.1 109.2 %copy-start.5 = (bf16[512,1024]{1,0:T(8,128)(2,1)S(1)}, bf16[512,1024]{1,0:T(8,128)(2,1)}, u32[]{:S(2)}) copy-start(bf16[512,1024]{1,0:T(8,128)(2,1)} %down_w.3) | copy-start | bytes 3145732

commit v2 on v1

--- a/solution.py
+++ b/solution.py
@@ -13,30 +13,58 @@
 NCH = 8
 T = 128
 H = 16
-LAG = dict(ax=-2, ac=-1, s1=0, s2=0, s3=1, s4=2, s5=3, s6=4, s7=5, s8=6)
-ORDER = ("ax", "ac", "s1", "s2", "s3", "s4", "s5", "s6", "s7", "s8")
-
-
-def apply_mask(w_ref, keep_ref):
-    cols = w_ref.shape[1]
-    shifts = lax.broadcasted_iota(jnp.int32, (16, cols), 0)
+ORDER = (
+    ("az", 3), ("az", 2), ("mask", 0), ("s1", 1), ("az", 4), ("ax", 3), ("ax", 2), ("s2", 1), ("az", 6),
+    ("s1", 0), ("ax", 4), ("ac", 3), ("az", 7), ("az", 5), ("s2", 0), ("s1", 3), ("ac", 2), ("ax", 6),
+    ("s1", 2), ("s3", 0), ("ac", 4), ("s3", 1), ("s2", 3), ("ax", 7), ("s1", 4), ("s2", 2), ("ac", 6),
+    ("s3", 3), ("s2", 4), ("s4", 0), ("ac", 7), ("s1", 6), ("ax", 5), ("s3", 4), ("s1", 7), ("s3", 2),
+    ("s2", 6), ("s4", 3), ("s5", 0), ("ac", 5), ("s4", 4), ("s3", 6), ("s1", 5), ("s2", 7), ("s5", 3),
+    ("s4", 2), ("s5", 4), ("s2", 5), ("s3", 7), ("s6", 3), ("s4", 6), ("s6", 4), ("s5", 2), ("s3", 5),
+    ("s4", 7), ("s7", 3), ("s5", 6), ("s7", 4), ("s7b", 3), ("s6", 2), ("s4", 5), ("s6", 6), ("s7", 2),
+    ("s5", 7), ("s7b", 4), ("s4", 1), ("s7b", 2), ("s5", 5), ("s8", 3), ("s6", 7), ("s7", 6), ("s8", 4),
+    ("s6", 0), ("s6", 5), ("s7b", 6), ("s7", 7), ("s5", 1), ("s7", 0), ("s8", 2), ("s7b", 7), ("s7", 5),
+    ("s8", 6), ("s6", 1), ("s7b", 0), ("s7b", 5), ("s8", 7), ("s7", 1), ("g", 1), ("s8", 5), ("s7b", 1),
+    ("g", 0), ("s8", 0), ("s9", 0), ("s8", 1), ("s9", 1), ("g", 2),
+)
+
+
+def unpack(keep_ref, i, shifts):
+    row = jnp.broadcast_to(keep_ref[pl.ds(i, 1), :], shifts.shape)
+    return (jnp.right_shift(row, shifts) & 1).astype(F32)
+
+
+def for_row_groups(keep_ref, body):
+    shifts = lax.broadcasted_iota(jnp.int32, (16, keep_ref.shape[1]), 0)
 
     def one(i, _):
-        row = jnp.broadcast_to(keep_ref[pl.ds(i, 1), :], (16, cols))
-        bits = (jnp.right_shift(row, shifts) & 1).astype(F32)
-        at = pl.ds(pl.multiple_of(i * 16, 16), 16)
-        w_ref[at, :] = (w_ref[at, :].astype(F32) * bits).astype(BF)
+        body(pl.ds(pl.multiple_of(i * 16, 16), 16), unpack(keep_ref, i, shifts))
         return 0
 
     lax.fori_loop(0, keep_ref.shape[0], one, 0, unroll=4)
+
+
+def apply_mask(w_ref, keep_ref, eff_ref):
+    def body(at, bits):
+        eff_ref[at, :] = (w_ref[at, :].astype(F32) * bits).astype(BF)
+
+    for_row_groups(keep_ref, body)
+
+
+def finish(full_ref, w_ref, keep_ref, grad_ref, score_ref):
+    def body(at, bits):
+        full = full_ref[at, :]
+        grad_ref[at, :] = (full * bits).astype(BF)
+        score_ref[at, :] = (-(w_ref[at, :].astype(F32) * full)).astype(BF)
+
+    for_row_groups(keep_ref, body)
 
 
 def comm_kernel(
     tokens, cot, gate_w, up_w, down_w, gate_k, up_k, down_k,
-    out, tc_out, g_out,
-    tc, gw, uw, dw, gk, uk, dk, pre, pre32, rx1, acc, rx3, hs, hr, keep, act,
-    dpart, d32, dr, zown, zs, zr, obuf,
-    ld_sem, send_sem, az, ax, ac, s1, s3, hrs, gh, gy, drs, zrs, ors, st_sem,
+    obuf, gate_g, up_g, down_g, gate_s, up_s, down_s,
+    tc, gr, ur, dr_w, gw, uw, dw, gk, uk, dk, pre, pre32, rx1, acc, rx3, hs, hr, keep, act,
+    dpart, d32, dk32, dr, zown, zs, zr, full, tall,
+    ld_sem, send_sem, az, ax, ac, s1, s3, hrs, gh, gy, dks, drs, zrs, ors,
 ):
     t = lax.axis_index("tok")
     r = lax.axis_index("row")
@@ -57,8 +85,8 @@
         for n, (src, dst) in enumerate(
             (
                 (tokens, tc.at[0, mine]), (cot, tc.at[1, mine]),
-                (gate_k, gk), (gate_w, gw), (up_k, uk), (up_w, uw),
-                (down_k, dk), (down_w, dw),
+                (gate_k, gk), (gate_w, gr), (up_k, uk), (up_w, ur),
+                (down_k, dk), (down_w, dr_w),
             )
         )
     ]
@@ -72,7 +100,7 @@
     for peer in peers:
         pl.semaphore_signal(barrier, inc=1, device_id=peer, device_id_type=MESH)
 
-    SEND = dict(az=0, ax=1, ac=2, rs=3, ag=4, d=5, z=6, o=7)
+    SEND = dict(az=0, ax=1, ac=2, rs=3, ag=4, d=5, z=6, o=7, dk=8)
 
     def send(src, dst, cls, recv, peer):
         pltpu.make_async_remote_copy(
@@ -187,15 +215,24 @@
             act[at, pl.ds(1024, 512)], uw[...], nt, preferred_element_type=F32
         )
         d32[i] = part
-        dpart[at, :] = part.astype(BF)
-        for n in range(7):
-            peer = (c + n + 1) % 8
-            send(dpart.at[rows(i, peer)], dr.at[i, n], "d", drs.at[i], (t, r, peer))
+        other = pl.ds(pl.multiple_of((1 - k) * 64, 64), 64)
+        send(d32.at[i, other], dk32.at[i], "dk", dks.at[i], at_core)
+
+    def stage_s7b(i):
+        wait(dk32.at[i], dks.at[i])
+        own = pl.ds(pl.multiple_of(k * 64, 64), 64)
+        part = d32[i, own, :] + dk32[i]
+        dk32[i] = part
+        dpart[i] = part.astype(BF)
+        for n in (1, 3, 2):
+            peer = (x + n) % 4
+            at = pl.ds(pl.multiple_of(peer * H, H), H)
+            send(dpart.at[i, at], dr.at[i, n - 1], "d", drs.at[i], (t, r, peer * 2 + k))
 
     def stage_s8(i):
         wait(dr.at[i], drs.at[i])
-        total = d32[i, pl.ds(pl.multiple_of(c * H, H), H), :]
-        for n in range(7):
+        total = dk32[i, pl.ds(pl.multiple_of(x * H, H), H), :]
+        for n in range(3):
             total = total + dr[i, n].astype(F32)
         if i < 2:
             zown[i] = total
@@ -208,93 +245,86 @@
         for n in range(3):
             wait(zr.at[2 * n + u], zrs.at[2 * n + u])
             total = total + zr[2 * n + u]
-        at = pl.ds(pl.multiple_of(u * T + c * H, H), H)
+        at = pl.ds(pl.multiple_of(u * T + (k * 4 + x) * H, H), H)
         obuf[at, :] = total.astype(BF)
         for n in range(7):
             send(obuf.at[at], obuf.at[at], "o", ors.at[u], (t, r, (c + n + 1) % 8))
 
+    tn = (((0,), (0,)), ((), ()))
+
+    def stage_g(n):
+        if n == 2:
+            tall[...] = lax.dot_general(
+                act[:, pl.ds(0, 512)], tc[1], tn, preferred_element_type=F32
+            )
+            finish(tall, dr_w, dk, down_g, down_s)
+            return
+        full[...] = lax.dot_general(
+            tc[0], act[:, pl.ds(512 * (n + 1), 512)], tn, preferred_element_type=F32
+        )
+        if n == 0:
+            finish(full, gr, gk, gate_g, gate_s)
+        else:
+            finish(full, ur, uk, up_g, up_s)
+
+    def stage_mask(_):
+        for n, (w, kk, eff) in enumerate(((gr, gk, gw), (ur, uk, uw), (dr_w, dk, dw))):
+            loads[2 + 2 * n].wait()
+            loads[3 + 2 * n].wait()
+            apply_mask(w, kk, eff)
+
     loads[0].wait()
     loads[1].wait()
     pl.semaphore_wait(barrier, len(peers))
-    for i in range(2, NCH):
-        stage_az(i)
-    for n, (w, kk) in enumerate(((gw, gk), (uw, uk), (dw, dk))):
-        loads[2 + 2 * n].wait()
-        loads[3 + 2 * n].wait()
-        apply_mask(w, kk)
-
     stages = dict(
-        ax=stage_ax, ac=stage_ac, s1=stage_s1, s2=stage_s2, s3=stage_s3, s4=stage_s4,
-        s5=stage_s5, s6=stage_s6, s7=stage_s7, s8=stage_s8,
+        az=stage_az, mask=stage_mask, ax=stage_ax, ac=stage_ac, s1=stage_s1, s2=stage_s2,
+        s3=stage_s3, s4=stage_s4, s5=stage_s5, s6=stage_s6, s7=stage_s7, s7b=stage_s7b,
+        s8=stage_s8, s9=stage_s9, g=stage_g,
     )
-    for tick in range(min(LAG.values()), NCH + max(LAG.values())):
-        for name in ORDER:
-            i = tick - LAG[name]
-            if 0 <= i < NCH:
-                stages[name](i)
-                if name == "s7" and i == NCH - 1:
-                    stores = [
-                        pltpu.make_async_copy(tc, tc_out, st_sem.at[0]),
-                        pltpu.make_async_copy(act, g_out, st_sem.at[1]),
-                    ]
-                    for copy in stores:
-                        copy.start()
-                if name == "s8" and i >= NCH - 2:
-                    stage_s9(i - (NCH - 2))
+    for name, i in ORDER:
+        stages[name](i)
     for u in range(2):
         wait(obuf.at[pl.ds(0, 7 * H)], ors.at[u])
-    last = pltpu.make_async_copy(obuf, out, st_sem.at[2])
-    last.start()
-    for copy in stores + [last]:
-        copy.wait()
     wait(tc.at[0, pl.ds(0, 6 * 32)], send_sem.at[0])
     wait(tc.at[0, pl.ds(0, 18 * 32)], send_sem.at[1])
     wait(tc.at[0, pl.ds(0, 6 * T)], send_sem.at[2])
     wait(pre.at[pl.ds(0, 56 * H)], send_sem.at[3])
     wait(act.at[pl.ds(0, 56 * H)], send_sem.at[4])
-    wait(dpart.at[pl.ds(0, 56 * H)], send_sem.at[5])
+    wait(dpart.at[pl.ds(0, 6)], send_sem.at[5])
     wait(zs, send_sem.at[6])
     wait(obuf.at[pl.ds(0, 14 * H)], send_sem.at[7])
-
-
-def grad_kernel(
-    tok, cot, hidden, gate_back, up_back, gate_w, up_w, down_w, gate_k, up_k, down_k,
-    gate_g, up_g, down_g, gate_s, up_s, down_s,
-):
-    def finish(full, w_ref, keep_ref, g_ref, s_ref):
-        n, cols = keep_ref.shape
-        shifts = lax.broadcasted_iota(jnp.int32, (16, cols), 0)
-        s_ref[...] = (-(w_ref[...].astype(F32) * full)).astype(BF)
-        for i in range(n):
-            row = jnp.broadcast_to(keep_ref[i : i + 1, :], (16, cols))
-            bits = (jnp.right_shift(row, shifts) & 1).astype(F32)
-            g_ref[16 * i : 16 * i + 16, :] = (full[16 * i : 16 * i + 16, :] * bits).astype(BF)
-
-    tn = (((0,), (0,)), ((), ()))
-    left = tok[0]
-    full = lax.dot_general(left, gate_back[...], tn, preferred_element_type=F32)
-    finish(full, gate_w, gate_k, gate_g, gate_s)
-    full = lax.dot_general(left, up_back[...], tn, preferred_element_type=F32)
-    finish(full, up_w, up_k, up_g, up_s)
-    full = lax.dot_general(hidden[...], cot[0], tn, preferred_element_type=F32)
-    finish(full, down_w, down_k, down_g, down_s)
-
-
-def on_device(tokens, cot, gate_w, up_w, down_w, gate_k, up_k, down_k):
-    any_spec = pl.BlockSpec(memory_space=pltpu.HBM)
+    wait(dk32, send_sem.at[8])
+
+
+def store_kernel(*refs):
+    n = len(refs) // 2
+    sems = refs[-1]
+    copies = [
+        pltpu.make_async_copy(refs[i], refs[n + i], sems.at[i]) for i in range(n)
+    ]
+    for copy in copies:
+        copy.start()
+    for copy in copies:
+        copy.wait()
+
+
+def on_device(*args):
+    hbm = pl.BlockSpec(memory_space=pltpu.HBM)
+    vmem = pl.BlockSpec(memory_space=pltpu.VMEM)
     dma = pltpu.SemaphoreType.DMA
-    out, tc, act = pl.pallas_call(
+    shapes = ((256, 1024),) + ((1024, 512), (1024, 512), (512, 1024)) * 2
+    args = [pltpu.with_memory_space_constraint(a, pltpu.HBM) for a in args]
+    outs = pl.pallas_call(
         comm_kernel,
         name="exchange",
-        out_shape=(
-            jax.ShapeDtypeStruct((256, 1024), BF),
-            jax.ShapeDtypeStruct((2, 1024, 1024), BF),
-            jax.ShapeDtypeStruct((1024, 1536), BF),
-        ),
-        in_specs=[any_spec] * 8,
-        out_specs=(any_spec,) * 3,
+        out_shape=[pltpu.VMEM(s, BF) for s in shapes],
+        in_specs=[hbm] * 8,
+        out_specs=[vmem] * 7,
         scratch_shapes=[
             pltpu.VMEM((2, 1024, 1024), BF),
+            pltpu.VMEM((1024, 512), BF),
+            pltpu.VMEM((1024, 512), BF),
+            pltpu.VMEM((512, 1024), BF),
             pltpu.VMEM((1024, 512), BF),
             pltpu.VMEM((1024, 512), BF),
             pltpu.VMEM((512, 1024), BF),
@@ -310,15 +340,17 @@
             pltpu.VMEM((NCH, H, 1536), BF),
             pltpu.VMEM((NCH, H, 1536), F32),
             pltpu.VMEM((1024, 1536), BF),
-            pltpu.VMEM((1024, 1024), BF),
+            pltpu.VMEM((NCH, 64, 1024), BF),
             pltpu.VMEM((NCH, T, 1024), F32),
-            pltpu.VMEM((NCH, 7, H, 1024), BF),
+            pltpu.VMEM((NCH, 64, 1024), F32),
+            pltpu.VMEM((NCH, 3, H, 1024), BF),
             pltpu.VMEM((2, H, 1024), F32),
             pltpu.VMEM((6, H, 1024), F32),
             pltpu.VMEM((6, H, 1024), F32),
-            pltpu.VMEM((256, 1024), BF),
+            pltpu.VMEM((1024, 512), F32),
+            pltpu.VMEM((512, 1024), F32),
             dma((8,)),
-            dma((8,)),
+            dma((9,)),
             dma((NCH,)),
             dma((NCH,)),
             dma((NCH,)),
@@ -327,40 +359,26 @@
             dma((NCH,)),
             dma((NCH,)),
             dma((NCH, 2)),
+            dma((NCH,)),
             dma((NCH,)),
             dma((6,)),
             dma((2,)),
-            dma((3,)),
         ],
         compiler_params=pltpu.CompilerParams(
-            collective_id=0, has_side_effects=True, vmem_limit_bytes=48 * 2**20
+            collective_id=0, has_side_effects=True, vmem_limit_bytes=50 * 2**20
         ),
-    )(tokens, cot, gate_w, up_w, down_w, gate_k, up_k, down_k)
-
-    n = 4
-    wide = pl.BlockSpec((1024 // n, 512), lambda i: (i, 0))
-    tall = pl.BlockSpec((512 // n, 1024), lambda i: (i, 0))
-    wide_keep = pl.BlockSpec((64 // n, 512), lambda i: (i, 0))
-    tall_keep = pl.BlockSpec((32 // n, 1024), lambda i: (i, 0))
-    up_shape = jax.ShapeDtypeStruct((1024, 512), BF)
-    down_shape = jax.ShapeDtypeStruct((512, 1024), BF)
-    grads = pl.pallas_call(
-        grad_kernel,
-        name="weight_grads",
-        grid=(n,),
-        out_shape=(up_shape, up_shape, down_shape) * 2,
-        in_specs=[
-            pl.BlockSpec((1, 1024, 1024 // n), lambda i: (0, 0, i)),
-            pl.BlockSpec((1, 1024, 1024), lambda i: (1, 0, 0)),
-            pl.BlockSpec((1024, 512 // n), lambda i: (0, i)),
-            pl.BlockSpec((1024, 512), lambda i: (0, 1)),
-            pl.BlockSpec((1024, 512), lambda i: (0, 2)),
-            wide, wide, tall, wide_keep, wide_keep, tall_keep,
-        ],
-        out_specs=(wide, wide, tall) * 2,
-        compiler_params=pltpu.CompilerParams(vmem_limit_bytes=48 * 2**20),
-    )(tc, tc, act, act, act, gate_w, up_w, down_w, gate_k, up_k, down_k)
-    return (out, *grads)
+    )(*args)
+    return tuple(
+        pl.pallas_call(
+            store_kernel,
+            name="store",
+            out_shape=[jax.ShapeDtypeStruct(s, BF) for s in shapes],
+            in_specs=[vmem] * 7,
+            out_specs=[hbm] * 7,
+            scratch_shapes=[dma((7,))],
+            compiler_params=pltpu.CompilerParams(vmem_limit_bytes=2**20),
+        )(*[pltpu.with_memory_space_constraint(o, pltpu.VMEM) for o in outs])
+    )
 
 
 def solution(mesh):

time: 128 us -> 96.4 us (0.75)
  Pallas kernels: 118 us -> 95.7 us
  local copies, waits for them, and re-layouts: 9.26 us -> 0 us
    pallas_call x2, Pallas kernels: 118 us -> 95.7 us  [the longest x1 92.7 us: on_device(): pl.pallas_call(comm_kernel, name='exchange', out_shape=[pltpu.VMEM(s, BF)...]
    unnamed x23 -> x0, local copies, waits for them, and re-layouts: 9.26 us -> none
where the time goes in v2:
time: 96.4 us; the launch traced here: 96.3 us
  Pallas kernels  95.7 us (99%)
    pallas_call x1, Pallas kernels, on_device(): pl.pallas_call(comm_kernel, name='exchange', out_shape=[pltpu.VMEM(s, BF)...  92.7 us
    pallas_call x1, Pallas kernels, on_device(): pl.pallas_call(store_kernel, name='store', out_shape=[jax.ShapeDtypeStruc...  2.9 us

profile of v2, /device:TPU:1, one launch (start us, length us, event | category | flops | bytes accessed | tf_op | source)
XLA Modules:
  0.0 96.3 jit_solution(17311021696405550671)
XLA Ops:
  0.6 92.7 %exchange.1 = (bf16[256,1024]{1,0:T(8,128)(2,1)S(1)}, bf16[1024,512]{1,0:T(8,128)(2,1)S(1)}, bf16[1024,512]{1,0:T(8,128)(2,1)S(1)}, bf16[512,1024]{1,0:T(8,128)(...) custom-call(bf16[256,1024]{1,0:T(8,128)(2,1)} %tokens.1, ...), custom_call_target="tpu_custom_call" | custom-call | tf_op jit(solution)/shard_map/exchange/pallas_call | solution.py:317
  93.4 2.9 %store.1 = (bf16[256,1024]{1,0:T(8,128)(2,1)}, bf16[1024,512]{1,0:T(8,128)(2,1)}, bf16[1024,512]{1,0:T(8,128)(2,1)}, bf16[512,1024]{1,0:T(8,128)(2,1)}, bf16[102...) custom-call(bf16[256,1024]{1,0:T(8,128)(2,1)S(1)} %get-tuple-element.14.refs_0_, ...), custom_call_target="tpu_custom_call" | custom-call | tf_op jit(solution)/shard_map/store/pallas_call | solution.py:372

commit v3 on v2

v3 whole, which is shorter than its diff:
```python
import functools

import jax
import jax.numpy as jnp
from jax import lax
from jax.experimental import pallas as pl
from jax.experimental.pallas import tpu as pltpu
from jax.sharding import PartitionSpec as P

MESH = pl.DeviceIdType.MESH
BF = jnp.bfloat16
F32 = jnp.float32
NCH = 8
T = 128
H = 16
BLOCK = (0, 0, 1, 2, 2, 3, 3, 1)
HALF = (0, 1, 0, 0, 1, 0, 1, 1)
LAST = NCH - 1
ORDER = (
    ("s1", 0), ("ax", 2), ("s1", 1), ("ax", 3), ("s2", 0), ("ac", 2), ("ax", 4), ("s1", 2), ("s2", 1),
    ("s3", 0), ("ax", 5), ("ac", 3), ("s2", 2), ("s1", 3), ("ax", 6), ("ax", 7), ("ac", 4), ("s3", 1),
    ("s4", 0), ("ac", 5), ("s3", 2), ("s2", 3), ("s1", 4), ("s1", 5), ("ac", 6), ("s3", 3), ("s2", 4),
    ("s1", 6), ("ac", 7), ("s2", 5), ("s4", 2), ("s5", 0), ("s3", 4), ("s2", 6), ("s4", 3), ("s1", 7),
    ("s3", 5), ("s6", 0), ("s5", 2), ("s3", 6), ("s2", 7), ("s5", 3), ("s4", 4), ("s4", 5), ("s7", 0),
    ("s6", 2), ("s3", 7), ("s6", 3), ("s4", 6), ("s7b", 0), ("s5", 4), ("s4", 1), ("s7", 2), ("s5", 5),
    ("s7", 3), ("s6", 4), ("t4", 1), ("s7b", 2), ("s4", 7), ("s7b", 3), ("s5", 6), ("s6", 5), ("s7", 4),
    ("t4", 5), ("t4", 4), ("t4", 2), ("s6", 6), ("s7b", 4), ("s5", 7), ("s7", 5), ("s5", 1), ("t4", 0),
    ("s7", 6), ("s6", 7), ("s7b", 5), ("t5", 1), ("s8", 0), ("t4", 6), ("s6", 1), ("s8", 2), ("t4", 7),
    ("s7b", 6), ("t4", 3), ("s7", 7), ("s8", 3), ("s7", 1), ("t5", 2), ("s7b", 7), ("s8", 5), ("t5", 5),
    ("t5", 6), ("t5", 7), ("s7b", 1), ("s8", 4), ("t5", 3), ("t5", 0), ("t5", 4), ("t6", 1), ("s8", 6),
    ("s8", 7), ("s9", 0), ("t7", 1), ("t6", 2), ("t6", 5), ("t6", 7), ("t6", 3), ("t6", 6), ("t6", 0),
    ("t6", 4), ("s8", 1), ("s9", 1), ("t7", 2), ("g", 1), ("t7", 6), ("t7", 0), ("t7", 3), ("g", 0),
    ("t7", 7), ("t7", 5), ("t7", 4), ("g", 2),
)


def unpack(keep_ref, i, shifts):
    row = jnp.broadcast_to(keep_ref[pl.ds(i, 1), :], shifts.shape)
    return (jnp.right_shift(row, shifts) & 1).astype(F32)


def for_row_groups(keep_ref, body):
    shifts = lax.broadcasted_iota(jnp.int32, (16, keep_ref.shape[1]), 0)

    def one(i, _):
        body(pl.ds(pl.multiple_of(i * 16, 16), 16), unpack(keep_ref, i, shifts))
        return 0

    lax.fori_loop(0, keep_ref.shape[0], one, 0, unroll=4)


def apply_mask(w_ref, keep_ref, eff_ref):
    def body(at, bits):
        eff_ref[at, :] = (w_ref[at, :].astype(F32) * bits).astype(BF)

    for_row_groups(keep_ref, body)


def finish(full_ref, w_ref, keep_ref, grad_ref, score_ref):
    def body(at, bits):
        full = full_ref[at, :]
        grad_ref[at, :] = (full * bits).astype(BF)
        score_ref[at, :] = (-(w_ref[at, :].astype(F32) * full)).astype(BF)

    for_row_groups(keep_ref, body)


def comm_kernel(
    tokens, cot, gate_w, up_w, down_w, gate_k, up_k, down_k,
    obuf, gate_g, up_g, down_g, gate_s, up_s, down_s,
    tc, gr, ur, dr_w, gw, uw, dw, gk, uk, dk, pre, pre32, rx1, acc, rx3, hs, hr, keep, act, hid,
    dpart, d32, dk32, dr, dr_last, zown, zs, zr, zs_last, zr_last, full, tall,
    ld_sem, send_sem, az, ax, ac, s1, s3, hrs, gh, gy, th, ty, dks, drs, zrs, ors,
):
    t = lax.axis_index("tok")
    r = lax.axis_index("row")
    c = lax.axis_index("col")
    rem = lax.rem
    h, k = rem(r, 2), rem(c, 2)
    y, x = lax.div(r, 2), lax.div(c, 2)
    y_next, y_prev, y_opp = rem(y + 1, 4), rem(y + 3, 4), rem(y + 2, 4)
    x_of = [rem(x + n, 4) for n in range(4)]
    x_col = [at_x * 2 + k for at_x in x_of]
    col_of = [rem(c + n, 8) for n in range(8)]
    at_next, at_prev = (t, y_next * 2 + h, c), (t, y_prev * 2 + h, c)
    at_twin = (t, y * 2 + (1 - h), c)
    at_core = (t, r, x * 2 + (1 - k))

    t0, t1 = rem(t, 2), lax.div(t, 2)
    tok_of = [rem(t0 + n % 2, 2) + 2 * rem(t1 + n // 2, 2) for n in range(4)]
    base_of = [[pl.multiple_of(b * 256 + u * T, T) for u in range(2)] for b in tok_of]

    mine = pl.ds(pl.multiple_of(t * 256, 256), 256)
    loads = [
        pltpu.make_async_copy(src, dst, ld_sem.at[n])
        for n, (src, dst) in enumerate(
            (
                (tokens, tc.at[0, mine]), (cot, tc.at[1, mine]),
                (gate_k, gk), (gate_w, gr), (up_k, uk), (up_w, ur),
                (down_k, dk), (down_w, dr_w),
            )
        )
    ]
    for copy in loads:
        copy.start()

    barrier = pltpu.get_barrier_semaphore()
    peers = [at_next, at_prev, at_twin]
    peers += [(t, r, col_of[n]) for n in range(1, 8)]
    peers += [(tok_of[n], r, c) for n in range(1, 4)]
    for peer in peers:
        pl.semaphore_signal(barrier, inc=1, device_id=peer, device_id_type=MESH)

    SEND = dict(az=0, ax=1, ac=2, rs=3, ag=4, d=5, z=6, o=7, dk=8, dl=9, zl=10, t=11)

    def send(src, dst, cls, recv, peer):
        pltpu.make_async_remote_copy(
            src_ref=src, dst_ref=dst, send_sem=send_sem.at[SEND[cls]], recv_sem=recv,
            device_id=peer, device_id_type=MESH,
        ).start()

    def wait(ref, sem):
        pltpu.make_async_copy(ref, ref, sem).wait()

    def base(i):
        return base_of[BLOCK[i]][HALF[i]]

    def rows(i, q, n=H):
        return pl.ds(pl.multiple_of(base(i) + q * n, n), n)

    def stage_az(i):
        for n in (0, 2) if BLOCK[i] == 1 else (0,):
            start = base_of[0][HALF[i]] + x_of[n] * 32
            at = pl.ds(pl.multiple_of(start, 32), 32)
            send(tc.at[k, at], tc.at[k, at], "az", az.at[i], (tok_of[BLOCK[i]], r, c))

    def stage_ax(i):
        near = BLOCK[i] == 1
        at = rows(i, x, 32)
        wait(tc.at[k, pl.ds(0, 64 if near else 32)], az.at[i])
        for n in (1, 3) if near else (1, 3, 2):
            send(tc.at[k, at], tc.at[k, at], "ax", ax.at[i], (t, r, x_col[n]))

    def stage_ac(i):
        wait(tc.at[k, pl.ds(0, 64 if BLOCK[i] == 1 else 96)], ax.at[i])
        at = rows(i, 0, T)
        send(tc.at[k, at], tc.at[k, at], "ac", ac.at[i], at_core)

    def forward(i, n):
        at = rows(i, 0, T)
        if n == 2:
            part = lax.dot_general(
                tc[1, at, :], dw[...], (((1,), (1,)), ((), ())), preferred_element_type=F32
            )
        else:
            part = jnp.dot(tc[0, at, :], (gw, uw)[n][...], preferred_element_type=F32)
        pre32[at, pl.ds(n * 512, 512)] = part
        pre[at, pl.ds(n * 512, 512)] = part.astype(BF)

    def stage_s1(i):
        if BLOCK[i]:
            wait(tc.at[1 - k, rows(i, 0, T)], ac.at[i])
        if i:
            for n in range(3):
                forward(i, n)
        send(pre.at[rows(i, y_opp * 2)], rx1.at[i, 0], "rs", s1.at[i], at_next)
        send(pre.at[rows(i, y_opp * 2 + 1)], rx1.at[i, 1], "rs", s1.at[i], at_prev)
        send(pre.at[rows(i, y_next * 2 + 1)], rx3.at[i, 0], "rs", s3.at[i], at_next)
        send(pre.at[rows(i, y_prev * 2)], rx3.at[i, 1], "rs", s3.at[i], at_prev)

    def stage_s2(i):
        wait(rx1.at[i], s1.at[i])
        acc[i, 0] = (rx1[i, 0].astype(F32) + pre32[rows(i, y_next * 2), :]).astype(BF)
        send(acc.at[i, 0], rx3.at[i, 2], "rs", s3.at[i], at_next)
        acc[i, 1] = (rx1[i, 1].astype(F32) + pre32[rows(i, y_prev * 2 + 1), :]).astype(BF)
        send(acc.at[i, 1], rx3.at[i, 3], "rs", s3.at[i], at_prev)

    def stage_s3(i):
        wait(rx3.at[i], s3.at[i])

        def total(half):
            return (
                pre32[rows(i, y * 2 + half), :]
                + rx3[i, 1 - half].astype(F32)
                + rx3[i, 2 + half].astype(F32)
            )

        hs[i] = total(1 - h).astype(BF)
        send(hs.at[i], hr.at[i], "rs", hrs.at[i], at_twin)
        keep[i] = total(h)

    def stage_s4(i):
        wait(hr.at[i], hrs.at[i])
        sums = keep[i] + hr[i].astype(F32)
        gate, up, back = sums[:, :512], sums[:, 512:1024], sums[:, 1024:]
        sig = jax.nn.sigmoid(gate)
        silu = gate * sig
        at = rows(i, r)
        hid[at, :] = (silu * up).astype(BF)
        act[at, pl.ds(0, 512)] = (back * up * (sig * (1.0 + gate * (1.0 - sig)))).astype(BF)
        act[at, pl.ds(512, 512)] = (back * silu).astype(BF)
        gather_own(i, act, "ag", gh, gy)

    def gather_own(i, ref, cls, twin_sem, ring_sem):
        at = rows(i, r)
        send(ref.at[at], ref.at[at], cls, twin_sem.at[i], at_twin)
        send(ref.at[at], ref.at[at], cls, ring_sem.at[i, h], at_next)
        send(ref.at[at], ref.at[at], cls, ring_sem.at[i, 1 - h], at_prev)

    def gather_twin(i, ref, cls, twin_sem, ring_sem):
        at = rows(i, y * 2 + (1 - h))
        wait(ref.at[at], twin_sem.at[i])
        send(ref.at[at], ref.at[at], cls, ring_sem.at[i, 1 - h], at_next)
        send(ref.at[at], ref.at[at], cls, ring_sem.at[i, h], at_prev)

    def gather_far(i, ref, cls, ring_sem):
        wait(ref.at[pl.ds(0, 2 * H)], ring_sem.at[i, 0])
        at = rows(i, y_prev * 2)
        send(ref.at[at], ref.at[at], cls, ring_sem.at[i, 1], at_next)
        at = rows(i, y_next * 2 + 1)
        send(ref.at[at], ref.at[at], cls, ring_sem.at[i, 1], at_prev)

    def stage_s5(i):
        gather_twin(i, act, "ag", gh, gy)

    def stage_s6(i):
        gather_far(i, act, "ag", gy)

    def stage_t4(i):
        gather_own(i, hid, "t", th, ty)

    def stage_t5(i):
        gather_twin(i, hid, "t", th, ty)

    def stage_t6(i):
        gather_far(i, hid, "t", ty)

    def stage_t7(i):
        wait(hid.at[pl.ds(0, 4 * H)], ty.at[i, 1])

    def stage_s7(i):
        wait(act.at[pl.ds(0, 4 * H)], gy.at[i, 1])
        at = rows(i, 0, T)
        nt = (((1,), (1,)), ((), ()))
        part = lax.dot_general(
            act[at, pl.ds(0, 512)], gw[...], nt, preferred_element_type=F32
        ) + lax.dot_general(
            act[at, pl.ds(512, 512)], uw[...], nt, preferred_element_type=F32
        )
        d32[i] = part
        other = pl.ds(pl.multiple_of((1 - k) * 64, 64), 64)
        send(d32.at[i, other], dk32.at[i], "dk", dks.at[i], at_core)

    def stage_s7b(i):
        wait(dk32.at[i], dks.at[i])
        own = pl.ds(pl.multiple_of(k * 64, 64), 64)
        part = d32[i, own, :] + dk32[i]
        dk32[i] = part
        if i == LAST:
            dpart[...] = part.astype(BF)
        for n in (1, 3, 2):
            at = pl.ds(pl.multiple_of(x_of[n] * H, H), H)
            to = (t, r, x_col[n])
            if i == LAST:
                send(dpart.at[at], dr_last.at[n - 1], "dl", drs.at[i], to)
            else:
                send(dk32.at[i, at], dr.at[i, n - 1], "d", drs.at[i], to)

    def stage_s8(i):
        came = dr_last if i == LAST else dr.at[i]
        wait(came, drs.at[i])
        total = dk32[i, pl.ds(pl.multiple_of(x * H, H), H), :]
        for n in range(3):
            total = total + came[n].astype(F32)
        b, u = BLOCK[i], HALF[i]
        if b == 0:
            zown[u] = total
        elif i == LAST:
            zs_last[...] = total
            send(zs_last, zr_last, "zl", zrs.at[u, b], (tok_of[b], r, c))
        else:
            zs[u, b] = total.astype(BF)
            send(zs.at[u, b], zr.at[u, b], "z", zrs.at[u, b], (tok_of[b], r, c))

    def stage_s9(u):
        total = zown[u]
        for b in range(1, 4):
            came = zr_last if (b, u) == (BLOCK[LAST], HALF[LAST]) else zr.at[u, b]
            wait(came, zrs.at[u, b])
            total = total + came[...].astype(F32)
        at = pl.ds(pl.multiple_of(u * T + (k * 4 + x) * H, H), H)
        obuf[at, :] = total.astype(BF)
        for n in range(7):
            send(obuf.at[at], obuf.at[at], "o", ors.at[u], (t, r, col_of[n + 1]))

    tn = (((0,), (0,)), ((), ()))

    def stage_g(n):
        if n == 2:
            tall[...] = lax.dot_general(
                hid[...], tc[1], tn, preferred_element_type=F32
            )
            finish(tall, dr_w, dk, down_g, down_s)
            return
        full[...] = lax.dot_general(
            tc[0], act[:, pl.ds(512 * n, 512)], tn, preferred_element_type=F32
        )
        if n == 0:
            finish(full, gr, gk, gate_g, gate_s)
        else:
            finish(full, ur, uk, up_g, up_s)

    def prepare(n):
        loads[2 + 2 * n].wait()
        loads[3 + 2 * n].wait()
        apply_mask((gr, ur, dr_w)[n], (gk, uk, dk)[n], (gw, uw, dw)[n])
        forward(0, n)

    loads[0].wait()
    loads[1].wait()
    prepare(0)
    pl.semaphore_wait(barrier, len(peers))
    for i in range(NCH):
        if BLOCK[i]:
            stage_az(i)
    prepare(1)
    prepare(2)
    stages = dict(
        ax=stage_ax, ac=stage_ac, s1=stage_s1, s2=stage_s2, s3=stage_s3, s4=stage_s4,
        s5=stage_s5, s6=stage_s6, s7=stage_s7, s7b=stage_s7b, s8=stage_s8, t4=stage_t4,
        t5=stage_t5, t6=stage_t6, t7=stage_t7, s9=stage_s9, g=stage_g,
    )
    for name, i in ORDER:
        stages[name](i)
    for u in range(2):
        wait(obuf.at[pl.ds(0, 7 * H)], ors.at[u])
    wait(tc.at[0, pl.ds(0, 8 * 32)], send_sem.at[0])
    wait(tc.at[0, pl.ds(0, 16 * 32)], send_sem.at[1])
    wait(tc.at[0, pl.ds(0, 6 * T)], send_sem.at[2])
    wait(pre.at[pl.ds(0, 56 * H)], send_sem.at[3])
    wait(act.at[pl.ds(0, 56 * H)], send_sem.at[4])
    wait(dr, send_sem.at[5])
    n_far = sum(1 for i in range(LAST) if BLOCK[i])
    wait(obuf.at[pl.ds(0, n_far * H)], send_sem.at[6])
    wait(obuf.at[pl.ds(0, 14 * H)], send_sem.at[7])
    wait(dk32, send_sem.at[8])
    wait(dr_last, send_sem.at[9])
    if BLOCK[LAST]:
        wait(zs_last, send_sem.at[10])
    wait(hid.at[pl.ds(0, 56 * H)], send_sem.at[11])


def store_kernel(*refs):
    n = len(refs) // 2
    sems = refs[-1]
    copies = [
        pltpu.make_async_copy(refs[i], refs[n + i], sems.at[i]) for i in range(n)
    ]
    for copy in copies:
        copy.start()
    for copy in copies:
        copy.wait()


def on_device(*args):
    hbm = pl.BlockSpec(memory_space=pltpu.HBM)
    vmem = pl.BlockSpec(memory_space=pltpu.VMEM)
    dma = pltpu.SemaphoreType.DMA
    shapes = ((256, 1024),) + ((1024, 512), (1024, 512), (512, 1024)) * 2
    args = [pltpu.with_memory_space_constraint(a, pltpu.HBM) for a in args]
    outs = pl.pallas_call(
        comm_kernel,
        name="exchange",
        out_shape=[pltpu.VMEM(s, BF) for s in shapes],
        in_specs=[hbm] * 8,
        out_specs=[vmem] * 7,
        scratch_shapes=[
            pltpu.VMEM((2, 1024, 1024), BF),
            pltpu.VMEM((1024, 512), BF),
            pltpu.VMEM((1024, 512), BF),
            pltpu.VMEM((512, 1024), BF),
            pltpu.VMEM((1024, 512), BF),
            pltpu.VMEM((1024, 512), BF),
            pltpu.VMEM((512, 1024), BF),
            pltpu.VMEM((64, 512), jnp.int32),
            pltpu.VMEM((64, 512), jnp.int32),
            pltpu.VMEM((32, 1024), jnp.int32),
            pltpu.VMEM((1024, 1536), BF),
            pltpu.VMEM((1024, 1536), F32),
            pltpu.VMEM((NCH, 2, H, 1536), BF),
            pltpu.VMEM((NCH, 2, H, 1536), BF),
            pltpu.VMEM((NCH, 4, H, 1536), BF),
            pltpu.VMEM((NCH, H, 1536), BF),
            pltpu.VMEM((NCH, H, 1536), BF),
            pltpu.VMEM((NCH, H, 1536), F32),
            pltpu.VMEM((1024, 1024), BF),
            pltpu.VMEM((1024, 512), BF),
            pltpu.VMEM((64, 1024), BF),
            pltpu.VMEM((NCH, T, 1024), F32),
            pltpu.VMEM((NCH, 64, 1024), F32),
            pltpu.VMEM((LAST, 3, H, 1024), F32),
            pltpu.VMEM((3, H, 1024), BF),
            pltpu.VMEM((2, H, 1024), F32),
            pltpu.VMEM((2, 4, H, 1024), BF),
            pltpu.VMEM((2, 4, H, 1024), BF),
            pltpu.VMEM((H, 1024), F32),
            pltpu.VMEM((H, 1024), F32),
            pltpu.VMEM((1024, 512), F32),
            pltpu.VMEM((512, 1024), F32),
            dma((8,)),
            dma((12,)),
            dma((NCH,)),
            dma((NCH,)),
            dma((NCH,)),
            dma((NCH,)),
            dma((NCH,)),
            dma((NCH,)),
            dma((NCH,)),
            dma((NCH, 2)),
            dma((NCH,)),
            dma((NCH, 2)),
            dma((NCH,)),
            dma((NCH,)),
            dma((2, 4)),
            dma((2,)),
        ],
        compiler_params=pltpu.CompilerParams(
            collective_id=0, has_side_effects=True, vmem_limit_bytes=50 * 2**20
        ),
    )(*args)
    return tuple(
        pl.pallas_call(
            store_kernel,
            name="store",
            out_shape=[jax.ShapeDtypeStruct(s, BF) for s in shapes],
            in_specs=[vmem] * 7,
            out_specs=[hbm] * 7,
            scratch_shapes=[dma((7,))],
            compiler_params=pltpu.CompilerParams(vmem_limit_bytes=2**20),
        )(*[pltpu.with_memory_space_constraint(o, pltpu.VMEM) for o in outs])
    )


def solution(mesh):
    return jax.shard_map(
        on_device,
        mesh=mesh,
        in_specs=(
            P("tok", "row"),
            P("tok", "row"),
            P("row", ("tok", "col")),
            P("row", ("tok", "col")),
            P(("tok", "col"), "row"),
            P("row", ("tok", "col")),
            P("row", ("tok", "col")),
            P(("tok", "col"), "row"),
        ),
        out_specs=(
            P("tok", "row"),
            P("row", ("tok", "col")),
            P("row", ("tok", "col")),
            P(("tok", "col"), "row"),
            P("row", ("tok", "col")),
            P("row", ("tok", "col")),
            P(("tok", "col"), "row"),
        ),
        check_vma=False,
    )
```

time: 96.4 us -> 93.6 us (0.971)
  Pallas kernels: 95.7 us -> 92.9 us
    pallas_call x1, Pallas kernels: 92.7 us -> 90 us  [on_device(): pl.pallas_call(comm_kernel, name='exchange', out_shape=[pltpu.VMEM(s, BF)...]
where the time goes in v3:
time: 93.6 us; the launch traced here: 93.5 us
  Pallas kernels  92.9 us (99%)
    pallas_call x1, Pallas kernels, on_device(): pl.pallas_call(comm_kernel, name='exchange', out_shape=[pltpu.VMEM(s, BF)...  90 us
    pallas_call x1, Pallas kernels, on_device(): pl.pallas_call(store_kernel, name='store', out_shape=[jax.ShapeDtypeStruc...  2.9 us

profile of v3, /device:TPU:1, one launch (start us, length us, event | category | flops | bytes accessed | tf_op | source)
XLA Modules:
  0.0 93.5 jit_solution(9077457028082475346)
XLA Ops:
  0.6 90.0 %exchange.1 = (bf16[256,1024]{1,0:T(8,128)(2,1)S(1)}, bf16[1024,512]{1,0:T(8,128)(2,1)S(1)}, bf16[1024,512]{1,0:T(8,128)(2,1)S(1)}, bf16[512,1024]{1,0:T(8,128)(...) custom-call(bf16[256,1024]{1,0:T(8,128)(2,1)} %tokens.1, ...), custom_call_target="tpu_custom_call" | custom-call | tf_op jit(solution)/shard_map/exchange/pallas_call | solution.py:371
  90.6 2.9 %store.1 = (bf16[256,1024]{1,0:T(8,128)(2,1)}, bf16[1024,512]{1,0:T(8,128)(2,1)}, bf16[1024,512]{1,0:T(8,128)(2,1)}, bf16[512,1024]{1,0:T(8,128)(2,1)}, bf16[102...) custom-call(bf16[256,1024]{1,0:T(8,128)(2,1)S(1)} %get-tuple-element.14.refs_0_, ...), custom_call_target="tpu_custom_call" | custom-call | tf_op jit(solution)/shard_map/store/pallas_call | solution.py:432

commit v4 on v3

--- a/solution.py
+++ b/solution.py
@@ -15,22 +15,23 @@
 H = 16
 BLOCK = (0, 0, 1, 2, 2, 3, 3, 1)
 HALF = (0, 1, 0, 0, 1, 0, 1, 1)
-LAST = NCH - 1
+WHOLE = (7,)
+NARROW = (0, 1, 7,)
 ORDER = (
-    ("s1", 0), ("ax", 2), ("s1", 1), ("ax", 3), ("s2", 0), ("ac", 2), ("ax", 4), ("s1", 2), ("s2", 1),
-    ("s3", 0), ("ax", 5), ("ac", 3), ("s2", 2), ("s1", 3), ("ax", 6), ("ax", 7), ("ac", 4), ("s3", 1),
-    ("s4", 0), ("ac", 5), ("s3", 2), ("s2", 3), ("s1", 4), ("s1", 5), ("ac", 6), ("s3", 3), ("s2", 4),
-    ("s1", 6), ("ac", 7), ("s2", 5), ("s4", 2), ("s5", 0), ("s3", 4), ("s2", 6), ("s4", 3), ("s1", 7),
-    ("s3", 5), ("s6", 0), ("s5", 2), ("s3", 6), ("s2", 7), ("s5", 3), ("s4", 4), ("s4", 5), ("s7", 0),
-    ("s6", 2), ("s3", 7), ("s6", 3), ("s4", 6), ("s7b", 0), ("s5", 4), ("s4", 1), ("s7", 2), ("s5", 5),
-    ("s7", 3), ("s6", 4), ("t4", 1), ("s7b", 2), ("s4", 7), ("s7b", 3), ("s5", 6), ("s6", 5), ("s7", 4),
-    ("t4", 5), ("t4", 4), ("t4", 2), ("s6", 6), ("s7b", 4), ("s5", 7), ("s7", 5), ("s5", 1), ("t4", 0),
-    ("s7", 6), ("s6", 7), ("s7b", 5), ("t5", 1), ("s8", 0), ("t4", 6), ("s6", 1), ("s8", 2), ("t4", 7),
-    ("s7b", 6), ("t4", 3), ("s7", 7), ("s8", 3), ("s7", 1), ("t5", 2), ("s7b", 7), ("s8", 5), ("t5", 5),
-    ("t5", 6), ("t5", 7), ("s7b", 1), ("s8", 4), ("t5", 3), ("t5", 0), ("t5", 4), ("t6", 1), ("s8", 6),
-    ("s8", 7), ("s9", 0), ("t7", 1), ("t6", 2), ("t6", 5), ("t6", 7), ("t6", 3), ("t6", 6), ("t6", 0),
-    ("t6", 4), ("s8", 1), ("s9", 1), ("t7", 2), ("g", 1), ("t7", 6), ("t7", 0), ("t7", 3), ("g", 0),
-    ("t7", 7), ("t7", 5), ("t7", 4), ("g", 2),
+    ("s1", 0), ("s1", 1), ("ax", 2), ("s2", 0), ("ax", 3), ("ac", 2), ("ax", 4), ("s1", 2), ("s3", 0),
+    ("ax", 5), ("s2", 1), ("ac", 3), ("s2", 2), ("s1", 3), ("ax", 6), ("s3", 1), ("ac", 4), ("s4", 0),
+    ("s3", 2), ("ac", 5), ("s2", 3), ("s1", 4), ("s1", 5), ("s3", 3), ("ac", 6), ("s2", 4), ("s1", 6),
+    ("s2", 5), ("s5", 0), ("s4", 2), ("ax", 7), ("s3", 4), ("s2", 6), ("s4", 3), ("ac", 7), ("s3", 5),
+    ("s6", 0), ("s5", 2), ("s1", 7), ("s3", 6), ("s5", 3), ("s4", 4), ("s7", 0), ("s2", 7), ("s6", 2),
+    ("s4", 5), ("s6", 3), ("s7b", 0), ("s4", 6), ("s3", 7), ("s5", 4), ("s7", 2), ("s5", 5), ("s7", 3),
+    ("s7b", 2), ("s6", 4), ("t4", 6), ("s5", 6), ("s4", 1), ("s6", 5), ("t4", 3), ("s7b", 3), ("t4", 1),
+    ("s7", 4), ("s6", 6), ("s4", 7), ("t4", 0), ("s7b", 4), ("s7", 5), ("s5", 1), ("s7", 6), ("s7b", 5),
+    ("s6", 7), ("t4", 4), ("t4", 5), ("s6", 1), ("t5", 3), ("t4", 7), ("t5", 1), ("s7b", 6), ("t5", 6),
+    ("s8", 3), ("s7", 7), ("t4", 2), ("s7", 1), ("s7b", 7), ("s8", 5), ("t5", 4), ("t5", 5), ("s8", 2),
+    ("t6", 3), ("t6", 6), ("s8", 4), ("s7b", 1), ("t6", 7), ("t5", 0), ("s8", 6), ("t6", 4), ("t6", 5),
+    ("s8", 0), ("t5", 2), ("t6", 1), ("s8", 7), ("s9", 0), ("g", 1), ("t7", 5), ("t7", 7), ("s8", 1),
+    ("t7", 6), ("t7", 1), ("s9", 1), ("t7", 4), ("t6", 0), ("t6", 2), ("g", 0), ("t7", 0), ("t7", 3),
+    ("t7", 2), ("g", 2),
 )
 
 
@@ -69,7 +70,7 @@
     tokens, cot, gate_w, up_w, down_w, gate_k, up_k, down_k,
     obuf, gate_g, up_g, down_g, gate_s, up_s, down_s,
     tc, gr, ur, dr_w, gw, uw, dw, gk, uk, dk, pre, pre32, rx1, acc, rx3, hs, hr, keep, act, hid,
-    dpart, d32, dk32, dr, dr_last, zown, zs, zr, zs_last, zr_last, full, tall,
+    dpart, d32, dk32, dr, dr16, zown, zs, zr, zs32, zr32, full, tall,
     ld_sem, send_sem, az, ax, ac, s1, s3, hrs, gh, gy, th, ty, dks, drs, zrs, ors,
 ):
     t = lax.axis_index("tok")
@@ -185,24 +186,40 @@
                 + rx3[i, 2 + half].astype(F32)
             )
 
-        hs[i] = total(1 - h).astype(BF)
-        send(hs.at[i], hr.at[i], "rs", hrs.at[i], at_twin)
-        keep[i] = total(h)
+        if i in WHOLE:
+            for half in range(2):
+                part = total(half)
+                hs[i, pl.ds(half * H, H)] = part.astype(BF)
+                keep[i, pl.ds(half * H, H)] = part
+            send(hs.at[i], hr.at[i], "rs", hrs.at[i], at_twin)
+        else:
+            first = pl.ds(0, H)
+            hs[i, first] = total(1 - h).astype(BF)
+            send(hs.at[i, first], hr.at[i, first], "rs", hrs.at[i], at_twin)
+            keep[i, first] = total(h)
+
+    def own_rows(i):
+        return rows(i, y, 2 * H) if i in WHOLE else rows(i, r)
 
     def stage_s4(i):
-        wait(hr.at[i], hrs.at[i])
-        sums = keep[i] + hr[i].astype(F32)
+        got = pl.ds(0, 2 * H if i in WHOLE else H)
+        wait(hr.at[i, got], hrs.at[i])
+        sums = keep[i, got] + hr[i, got].astype(F32)
         gate, up, back = sums[:, :512], sums[:, 512:1024], sums[:, 1024:]
         sig = jax.nn.sigmoid(gate)
         silu = gate * sig
-        at = rows(i, r)
+        at = own_rows(i)
         hid[at, :] = (silu * up).astype(BF)
         act[at, pl.ds(0, 512)] = (back * up * (sig * (1.0 + gate * (1.0 - sig)))).astype(BF)
         act[at, pl.ds(512, 512)] = (back * silu).astype(BF)
         gather_own(i, act, "ag", gh, gy)
 
     def gather_own(i, ref, cls, twin_sem, ring_sem):
-        at = rows(i, r)
+        at = own_rows(i)
+        if i in WHOLE:
+            send(ref.at[at], ref.at[at], cls, ring_sem.at[i, 0], at_next)
+            send(ref.at[at], ref.at[at], cls, ring_sem.at[i, 0], at_prev)
+            return
         send(ref.at[at], ref.at[at], cls, twin_sem.at[i], at_twin)
         send(ref.at[at], ref.at[at], cls, ring_sem.at[i, h], at_next)
         send(ref.at[at], ref.at[at], cls, ring_sem.at[i, 1 - h], at_prev)
@@ -214,7 +231,7 @@
         send(ref.at[at], ref.at[at], cls, ring_sem.at[i, h], at_prev)
 
     def gather_far(i, ref, cls, ring_sem):
-        wait(ref.at[pl.ds(0, 2 * H)], ring_sem.at[i, 0])
+        wait(ref.at[pl.ds(0, (4 if i in WHOLE else 2) * H)], ring_sem.at[i, 0])
         at = rows(i, y_prev * 2)
         send(ref.at[at], ref.at[at], cls, ring_sem.at[i, 1], at_next)
         at = rows(i, y_next * 2 + 1)
@@ -236,10 +253,10 @@
         gather_far(i, hid, "t", ty)
 
     def stage_t7(i):
-        wait(hid.at[pl.ds(0, 4 * H)], ty.at[i, 1])
+        wait(hid.at[pl.ds(0, (2 if i in WHOLE else 4) * H)], ty.at[i, 1])
 
     def stage_s7(i):
-        wait(act.at[pl.ds(0, 4 * H)], gy.at[i, 1])
+        wait(act.at[pl.ds(0, (2 if i in WHOLE else 4) * H)], gy.at[i, 1])
         at = rows(i, 0, T)
         nt = (((1,), (1,)), ((), ()))
         part = lax.dot_general(
@@ -256,18 +273,18 @@
         own = pl.ds(pl.multiple_of(k * 64, 64), 64)
         part = d32[i, own, :] + dk32[i]
         dk32[i] = part
-        if i == LAST:
-            dpart[...] = part.astype(BF)
+        if i in NARROW:
+            dpart[i] = part.astype(BF)
         for n in (1, 3, 2):
             at = pl.ds(pl.multiple_of(x_of[n] * H, H), H)
             to = (t, r, x_col[n])
-            if i == LAST:
-                send(dpart.at[at], dr_last.at[n - 1], "dl", drs.at[i], to)
+            if i in NARROW:
+                send(dpart.at[i, at], dr16.at[i, n - 1], "dl", drs.at[i], to)
             else:
                 send(dk32.at[i, at], dr.at[i, n - 1], "d", drs.at[i], to)
 
     def stage_s8(i):
-        came = dr_last if i == LAST else dr.at[i]
+        came = dr16.at[i] if i in NARROW else dr.at[i]
         wait(came, drs.at[i])
         total = dk32[i, pl.ds(pl.multiple_of(x * H, H), H), :]
         for n in range(3):
@@ -275,9 +292,9 @@
         b, u = BLOCK[i], HALF[i]
         if b == 0:
             zown[u] = total
-        elif i == LAST:
-            zs_last[...] = total
-            send(zs_last, zr_last, "zl", zrs.at[u, b], (tok_of[b], r, c))
+        elif i in NARROW:
+            zs32[u, b] = total
+            send(zs32.at[u, b], zr32.at[u, b], "zl", zrs.at[u, b], (tok_of[b], r, c))
         else:
             zs[u, b] = total.astype(BF)
             send(zs.at[u, b], zr.at[u, b], "z", zrs.at[u, b], (tok_of[b], r, c))
@@ -285,7 +302,8 @@
     def stage_s9(u):
         total = zown[u]
         for b in range(1, 4):
-            came = zr_last if (b, u) == (BLOCK[LAST], HALF[LAST]) else zr.at[u, b]
+            narrow = any((BLOCK[i], HALF[i]) == (b, u) for i in NARROW)
+            came = (zr32 if narrow else zr).at[u, b]
             wait(came, zrs.at[u, b])
             total = total + came[...].astype(F32)
         at = pl.ds(pl.multiple_of(u * T + (k * 4 + x) * H, H), H)
@@ -337,17 +355,18 @@
     wait(tc.at[0, pl.ds(0, 8 * 32)], send_sem.at[0])
     wait(tc.at[0, pl.ds(0, 16 * 32)], send_sem.at[1])
     wait(tc.at[0, pl.ds(0, 6 * T)], send_sem.at[2])
-    wait(pre.at[pl.ds(0, 56 * H)], send_sem.at[3])
-    wait(act.at[pl.ds(0, 56 * H)], send_sem.at[4])
-    wait(dr, send_sem.at[5])
-    n_far = sum(1 for i in range(LAST) if BLOCK[i])
-    wait(obuf.at[pl.ds(0, n_far * H)], send_sem.at[6])
+    whole, narrow = len(WHOLE), len(NARROW)
+    wait(pre.at[pl.ds(0, (56 + whole) * H)], send_sem.at[3])
+    wait(act.at[pl.ds(0, (56 - whole) * H)], send_sem.at[4])
+    wait(dr.at[pl.ds(0, NCH - narrow)], send_sem.at[5])
+    far = sum(1 for i in range(NCH) if BLOCK[i] and i not in NARROW)
+    wait(obuf.at[pl.ds(0, far * H)], send_sem.at[6])
     wait(obuf.at[pl.ds(0, 14 * H)], send_sem.at[7])
     wait(dk32, send_sem.at[8])
-    wait(dr_last, send_sem.at[9])
-    if BLOCK[LAST]:
-        wait(zs_last, send_sem.at[10])
-    wait(hid.at[pl.ds(0, 56 * H)], send_sem.at[11])
+    wait(dr16.at[pl.ds(0, narrow)], send_sem.at[9])
+    if far < 6:
+        wait(dk32.at[0, pl.ds(0, (6 - far) * H)], send_sem.at[10])
+    wait(hid.at[pl.ds(0, (56 - whole) * H)], send_sem.at[11])
 
 
 def store_kernel(*refs):
@@ -390,21 +409,21 @@
             pltpu.VMEM((NCH, 2, H, 1536), BF),
             pltpu.VMEM((NCH, 2, H, 1536), BF),
             pltpu.VMEM((NCH, 4, H, 1536), BF),
-            pltpu.VMEM((NCH, H, 1536), BF),
-            pltpu.VMEM((NCH, H, 1536), BF),
-            pltpu.VMEM((NCH, H, 1536), F32),
+            pltpu.VMEM((NCH, 2 * H, 1536), BF),
+            pltpu.VMEM((NCH, 2 * H, 1536), BF),
+            pltpu.VMEM((NCH, 2 * H, 1536), F32),
             pltpu.VMEM((1024, 1024), BF),
             pltpu.VMEM((1024, 512), BF),
-            pltpu.VMEM((64, 1024), BF),
+            pltpu.VMEM((NCH, 64, 1024), BF),
             pltpu.VMEM((NCH, T, 1024), F32),
             pltpu.VMEM((NCH, 64, 1024), F32),
-            pltpu.VMEM((LAST, 3, H, 1024), F32),
-            pltpu.VMEM((3, H, 1024), BF),
+            pltpu.VMEM((NCH, 3, H, 1024), F32),
+            pltpu.VMEM((NCH, 3, H, 1024), BF),
             pltpu.VMEM((2, H, 1024), F32),
             pltpu.VMEM((2, 4, H, 1024), BF),
             pltpu.VMEM((2, 4, H, 1024), BF),
-            pltpu.VMEM((H, 1024), F32),
-            pltpu.VMEM((H, 1024), F32),
+            pltpu.VMEM((2, 4, H, 1024), F32),
+            pltpu.VMEM((2, 4, H, 1024), F32),
             pltpu.VMEM((1024, 512), F32),
             pltpu.VMEM((512, 1024), F32),
             dma((8,)),

time: 93.6 us -> 91.7 us (0.980)
  Pallas kernels: 92.9 us -> 91 us
    pallas_call x1, Pallas kernels: 90 us -> 88.1 us  [on_device(): pl.pallas_call(comm_kernel, name='exchange', out_shape=[pltpu.VMEM(s, BF)...]
where the time goes in v4:
time: 91.7 us; the launch traced here: 91.6 us
  Pallas kernels  91 us (99%)
    pallas_call x1, Pallas kernels, on_device(): pl.pallas_call(comm_kernel, name='exchange', out_shape=[pltpu.VMEM(s, BF)...  88.1 us
    pallas_call x1, Pallas kernels, on_device(): pl.pallas_call(store_kernel, name='store', out_shape=[jax.ShapeDtypeStruc...  2.9 us

profile of v4, /device:TPU:1, one launch (start us, length us, event | category | flops | bytes accessed | tf_op | source)
XLA Modules:
  0.0 91.6 jit_solution(17193697487887300978)
XLA Ops:
  0.6 88.1 %exchange.1 = (bf16[256,1024]{1,0:T(8,128)(2,1)S(1)}, bf16[1024,512]{1,0:T(8,128)(2,1)S(1)}, bf16[1024,512]{1,0:T(8,128)(2,1)S(1)}, bf16[512,1024]{1,0:T(8,128)(...) custom-call(bf16[256,1024]{1,0:T(8,128)(2,1)} %tokens.1, ...), custom_call_target="tpu_custom_call" | custom-call | tf_op jit(solution)/shard_map/exchange/pallas_call | solution.py:390
  88.7 2.9 %store.1 = (bf16[256,1024]{1,0:T(8,128)(2,1)}, bf16[1024,512]{1,0:T(8,128)(2,1)}, bf16[1024,512]{1,0:T(8,128)(2,1)}, bf16[512,1024]{1,0:T(8,128)(2,1)}, bf16[102...) custom-call(bf16[256,1024]{1,0:T(8,128)(2,1)S(1)} %get-tuple-element.14.refs_0_, ...), custom_call_target="tpu_custom_call" | custom-call | tf_op jit(solution)/shard_map/store/pallas_call | solution.py:451

commit v5 on v4

--- a/solution.py
+++ b/solution.py
@@ -13,25 +13,25 @@
 NCH = 8
 T = 128
 H = 16
-BLOCK = (0, 0, 1, 2, 2, 3, 3, 1)
-HALF = (0, 1, 0, 0, 1, 0, 1, 1)
+BLOCK = (0, 0, 1, 2, 3, 3, 2, 1)
+HALF = (0, 1, 0, 0, 0, 1, 1, 1)
 WHOLE = (7,)
 NARROW = (0, 1, 7,)
 ORDER = (
-    ("s1", 0), ("s1", 1), ("ax", 2), ("s2", 0), ("ax", 3), ("ac", 2), ("ax", 4), ("s1", 2), ("s3", 0),
-    ("ax", 5), ("s2", 1), ("ac", 3), ("s2", 2), ("s1", 3), ("ax", 6), ("s3", 1), ("ac", 4), ("s4", 0),
-    ("s3", 2), ("ac", 5), ("s2", 3), ("s1", 4), ("s1", 5), ("s3", 3), ("ac", 6), ("s2", 4), ("s1", 6),
-    ("s2", 5), ("s5", 0), ("s4", 2), ("ax", 7), ("s3", 4), ("s2", 6), ("s4", 3), ("ac", 7), ("s3", 5),
-    ("s6", 0), ("s5", 2), ("s1", 7), ("s3", 6), ("s5", 3), ("s4", 4), ("s7", 0), ("s2", 7), ("s6", 2),
-    ("s4", 5), ("s6", 3), ("s7b", 0), ("s4", 6), ("s3", 7), ("s5", 4), ("s7", 2), ("s5", 5), ("s7", 3),
-    ("s7b", 2), ("s6", 4), ("t4", 6), ("s5", 6), ("s4", 1), ("s6", 5), ("t4", 3), ("s7b", 3), ("t4", 1),
-    ("s7", 4), ("s6", 6), ("s4", 7), ("t4", 0), ("s7b", 4), ("s7", 5), ("s5", 1), ("s7", 6), ("s7b", 5),
-    ("s6", 7), ("t4", 4), ("t4", 5), ("s6", 1), ("t5", 3), ("t4", 7), ("t5", 1), ("s7b", 6), ("t5", 6),
-    ("s8", 3), ("s7", 7), ("t4", 2), ("s7", 1), ("s7b", 7), ("s8", 5), ("t5", 4), ("t5", 5), ("s8", 2),
-    ("t6", 3), ("t6", 6), ("s8", 4), ("s7b", 1), ("t6", 7), ("t5", 0), ("s8", 6), ("t6", 4), ("t6", 5),
-    ("s8", 0), ("t5", 2), ("t6", 1), ("s8", 7), ("s9", 0), ("g", 1), ("t7", 5), ("t7", 7), ("s8", 1),
-    ("t7", 6), ("t7", 1), ("s9", 1), ("t7", 4), ("t6", 0), ("t6", 2), ("g", 0), ("t7", 0), ("t7", 3),
-    ("t7", 2), ("g", 2),
+    ("s1", 0), ("ax", 2), ("s2", 0), ("az", 5), ("s1", 1), ("az", 7), ("ax", 3), ("ac", 2), ("ax", 4),
+    ("s3", 0), ("az", 6), ("s1", 2), ("s2", 1), ("ac", 3), ("ax", 5), ("s2", 2), ("s1", 3), ("ac", 4),
+    ("s4", 0), ("ax", 6), ("s3", 1), ("s1", 4), ("ac", 5), ("s3", 2), ("s2", 3), ("s1", 5), ("ax", 7),
+    ("s2", 4), ("ac", 6), ("s5", 0), ("s3", 3), ("s1", 6), ("ac", 7), ("s2", 5), ("s4", 2), ("s3", 4),
+    ("s2", 6), ("s4", 3), ("s3", 5), ("s6", 0), ("s5", 2), ("s1", 7), ("s3", 6), ("s4", 4), ("s5", 3),
+    ("s7", 0), ("s2", 7), ("s6", 2), ("s4", 5), ("s6", 3), ("s4", 6), ("s3", 7), ("s7b", 0), ("s5", 4),
+    ("s7", 2), ("s5", 5), ("s7", 3), ("s7b", 2), ("s6", 4), ("s5", 6), ("t4", 0), ("s7b", 3), ("s4", 1),
+    ("t4", 4), ("s6", 5), ("t4", 2), ("s7", 4), ("s6", 6), ("t4", 5), ("s4", 7), ("s8", 0), ("s7b", 4),
+    ("s7", 5), ("s5", 1), ("s7", 6), ("s7b", 5), ("s6", 7), ("t4", 6), ("s8", 2), ("s8", 3), ("s7b", 6),
+    ("s6", 1), ("t4", 1), ("t4", 3), ("t5", 4), ("t5", 0), ("s7", 7), ("s8", 4), ("s7", 1), ("s7b", 7),
+    ("t5", 5), ("t4", 7), ("s8", 5), ("t5", 6), ("t6", 0), ("s7b", 1), ("t5", 2), ("t5", 1), ("t5", 3),
+    ("t6", 4), ("s8", 6), ("t6", 5), ("s9", 0), ("s8", 7), ("t6", 6), ("t6", 2), ("g", 1), ("t6", 3),
+    ("t6", 1), ("s8", 1), ("t7", 2), ("s9", 1), ("t6", 7), ("t7", 5), ("t7", 3), ("g", 0), ("t7", 6),
+    ("t7", 1), ("t7", 4), ("t7", 0), ("t7", 7), ("g", 2),
 )
 
 
@@ -91,6 +91,13 @@
     tok_of = [rem(t0 + n % 2, 2) + 2 * rem(t1 + n // 2, 2) for n in range(4)]
     base_of = [[pl.multiple_of(b * 256 + u * T, T) for u in range(2)] for b in tok_of]
 
+    barrier = pltpu.get_barrier_semaphore()
+    peers = [at_next, at_prev, at_twin]
+    peers += [(t, r, col_of[n]) for n in range(1, 8)]
+    peers += [(tok_of[n], r, c) for n in range(1, 4)]
+    for peer in peers:
+        pl.semaphore_signal(barrier, inc=1, device_id=peer, device_id_type=MESH)
+
     mine = pl.ds(pl.multiple_of(t * 256, 256), 256)
     loads = [
         pltpu.make_async_copy(src, dst, ld_sem.at[n])
@@ -104,13 +111,6 @@
     ]
     for copy in loads:
         copy.start()
-
-    barrier = pltpu.get_barrier_semaphore()
-    peers = [at_next, at_prev, at_twin]
-    peers += [(t, r, col_of[n]) for n in range(1, 8)]
-    peers += [(tok_of[n], r, c) for n in range(1, 4)]
-    for peer in peers:
-        pl.semaphore_signal(barrier, inc=1, device_id=peer, device_id_type=MESH)
 
     SEND = dict(az=0, ax=1, ac=2, rs=3, ag=4, d=5, z=6, o=7, dk=8, dl=9, zl=10, t=11)
 
@@ -339,12 +339,12 @@
     prepare(0)
     pl.semaphore_wait(barrier, len(peers))
     for i in range(NCH):
-        if BLOCK[i]:
+        if BLOCK[i] and ("az", i) not in ORDER:
             stage_az(i)
     prepare(1)
     prepare(2)
     stages = dict(
-        ax=stage_ax, ac=stage_ac, s1=stage_s1, s2=stage_s2, s3=stage_s3, s4=stage_s4,
+        az=stage_az, ax=stage_ax, ac=stage_ac, s1=stage_s1, s2=stage_s2, s3=stage_s3, s4=stage_s4,
         s5=stage_s5, s6=stage_s6, s7=stage_s7, s7b=stage_s7b, s8=stage_s8, t4=stage_t4,
         t5=stage_t5, t6=stage_t6, t7=stage_t7, s9=stage_s9, g=stage_g,
     )

time: 91.7 us -> 90.2 us (0.984)
  Pallas kernels: 91 us -> 89.5 us
    pallas_call x1, Pallas kernels: 88.1 us -> 86.6 us  [on_device(): pl.pallas_call(comm_kernel, name='exchange', out_shape=[pltpu.VMEM(s, BF)...]
where the time goes in v5:
time: 90.2 us
  Pallas kernels  89.5 us (99%)
    pallas_call x1, Pallas kernels, on_device(): pl.pallas_call(comm_kernel, name='exchange', out_shape=[pltpu.VMEM(s, BF)...  86.6 us
    pallas_call x1, Pallas kernels, on_device(): pl.pallas_call(store_kernel, name='store', out_shape=[jax.ShapeDtypeStruc...  2.9 us

profile of v5, /device:TPU:1, one launch (start us, length us, event | category | flops | bytes accessed | tf_op | source)
XLA Modules:
  0.0 90.2 jit_solution(17650372257652371590)
XLA Ops:
  0.6 86.6 %exchange.1 = (bf16[256,1024]{1,0:T(8,128)(2,1)S(1)}, bf16[1024,512]{1,0:T(8,128)(2,1)S(1)}, bf16[1024,512]{1,0:T(8,128)(2,1)S(1)}, bf16[512,1024]{1,0:T(8,128)(...) custom-call(bf16[256,1024]{1,0:T(8,128)(2,1)} %tokens.1, ...), custom_call_target="tpu_custom_call" | custom-call | tf_op jit(solution)/shard_map/exchange/pallas_call | solution.py:390
  87.3 2.9 %store.1 = (bf16[256,1024]{1,0:T(8,128)(2,1)}, bf16[1024,512]{1,0:T(8,128)(2,1)}, bf16[1024,512]{1,0:T(8,128)(2,1)}, bf16[512,1024]{1,0:T(8,128)(2,1)}, bf16[102...) custom-call(bf16[256,1024]{1,0:T(8,128)(2,1)S(1)} %get-tuple-element.14.refs_0_, ...), custom_call_target="tpu_custom_call" | custom-call | tf_op jit(solution)/shard_map/store/pallas_call | solution.py:451

commit v6 on v5

--- a/solution.py
+++ b/solution.py
@@ -18,20 +18,20 @@
 WHOLE = (7,)
 NARROW = (0, 1, 7,)
 ORDER = (
-    ("s1", 0), ("ax", 2), ("s2", 0), ("az", 5), ("s1", 1), ("az", 7), ("ax", 3), ("ac", 2), ("ax", 4),
-    ("s3", 0), ("az", 6), ("s1", 2), ("s2", 1), ("ac", 3), ("ax", 5), ("s2", 2), ("s1", 3), ("ac", 4),
-    ("s4", 0), ("ax", 6), ("s3", 1), ("s1", 4), ("ac", 5), ("s3", 2), ("s2", 3), ("s1", 5), ("ax", 7),
-    ("s2", 4), ("ac", 6), ("s5", 0), ("s3", 3), ("s1", 6), ("ac", 7), ("s2", 5), ("s4", 2), ("s3", 4),
-    ("s2", 6), ("s4", 3), ("s3", 5), ("s6", 0), ("s5", 2), ("s1", 7), ("s3", 6), ("s4", 4), ("s5", 3),
-    ("s7", 0), ("s2", 7), ("s6", 2), ("s4", 5), ("s6", 3), ("s4", 6), ("s3", 7), ("s7b", 0), ("s5", 4),
-    ("s7", 2), ("s5", 5), ("s7", 3), ("s7b", 2), ("s6", 4), ("s5", 6), ("t4", 0), ("s7b", 3), ("s4", 1),
-    ("t4", 4), ("s6", 5), ("t4", 2), ("s7", 4), ("s6", 6), ("t4", 5), ("s4", 7), ("s8", 0), ("s7b", 4),
-    ("s7", 5), ("s5", 1), ("s7", 6), ("s7b", 5), ("s6", 7), ("t4", 6), ("s8", 2), ("s8", 3), ("s7b", 6),
-    ("s6", 1), ("t4", 1), ("t4", 3), ("t5", 4), ("t5", 0), ("s7", 7), ("s8", 4), ("s7", 1), ("s7b", 7),
-    ("t5", 5), ("t4", 7), ("s8", 5), ("t5", 6), ("t6", 0), ("s7b", 1), ("t5", 2), ("t5", 1), ("t5", 3),
-    ("t6", 4), ("s8", 6), ("t6", 5), ("s9", 0), ("s8", 7), ("t6", 6), ("t6", 2), ("g", 1), ("t6", 3),
-    ("t6", 1), ("s8", 1), ("t7", 2), ("s9", 1), ("t6", 7), ("t7", 5), ("t7", 3), ("g", 0), ("t7", 6),
-    ("t7", 1), ("t7", 4), ("t7", 0), ("t7", 7), ("g", 2),
+    ("s1", 0), ("s2", 0), ("az", 5), ("az", 6), ("ax", 2), ("s1", 1), ("ax", 3), ("s3", 0), ("ac", 2),
+    ("ax", 4), ("s2", 1), ("s1", 2), ("ac", 3), ("ax", 5), ("az", 7), ("s1", 3), ("s3", 1), ("ac", 4),
+    ("s2", 2), ("ax", 6), ("s1", 4), ("s2", 3), ("ac", 5), ("s4", 0), ("s3", 2), ("ax", 7), ("s1", 5),
+    ("ac", 6), ("s2", 4), ("s3", 3), ("s1", 6), ("s2", 5), ("s5", 0), ("s4", 2), ("s3", 4), ("s2", 6),
+    ("s4", 3), ("ac", 7), ("s3", 5), ("s5", 2), ("s6", 0), ("s1", 7), ("s3", 6), ("s5", 3), ("s6", 2),
+    ("s4", 4), ("s7", 0), ("s2", 7), ("s4", 5), ("s6", 3), ("s7b", 0), ("s4", 6), ("s7", 2), ("s5", 4),
+    ("s3", 7), ("s4", 1), ("t4", 4), ("s5", 5), ("s7b", 2), ("s7", 3), ("s8", 0), ("s6", 4), ("s5", 6),
+    ("t4", 2), ("t4", 6), ("s7b", 3), ("s6", 5), ("t4", 0), ("t4", 5), ("s7", 4), ("s6", 6), ("t4", 1),
+    ("s8", 2), ("s4", 7), ("s7b", 4), ("s7", 5), ("s5", 1), ("s7", 6), ("s8", 3), ("s7b", 5), ("s6", 7),
+    ("t4", 3), ("s7b", 6), ("s6", 1), ("t5", 5), ("t5", 6), ("t4", 7), ("t5", 0), ("t5", 2), ("t5", 1),
+    ("s7", 7), ("s8", 4), ("s7", 1), ("s8", 5), ("s7b", 7), ("t6", 0), ("t5", 4), ("t5", 3), ("s7b", 1),
+    ("t6", 7), ("t6", 5), ("t6", 2), ("s8", 6), ("s9", 0), ("s8", 7), ("t6", 6), ("g", 0), ("t6", 1),
+    ("t6", 4), ("t7", 6), ("s8", 1), ("t6", 3), ("s9", 1), ("t7", 7), ("g", 1), ("t7", 3), ("t7", 0),
+    ("t7", 4), ("t7", 2), ("t7", 5), ("t7", 1), ("g", 2),
 )
 
 
@@ -139,7 +139,7 @@
         near = BLOCK[i] == 1
         at = rows(i, x, 32)
         wait(tc.at[k, pl.ds(0, 64 if near else 32)], az.at[i])
-        for n in (1, 3) if near else (1, 3, 2):
+        for n in (1, 3) if near else (2, 1, 3):
             send(tc.at[k, at], tc.at[k, at], "ax", ax.at[i], (t, r, x_col[n]))
 
     def stage_ac(i):
@@ -275,7 +275,7 @@
         dk32[i] = part
         if i in NARROW:
             dpart[i] = part.astype(BF)
-        for n in (1, 3, 2):
+        for n in (2, 1, 3):
             at = pl.ds(pl.multiple_of(x_of[n] * H, H), H)
             to = (t, r, x_col[n])
             if i in NARROW:
@@ -308,8 +308,10 @@
             total = total + came[...].astype(F32)
         at = pl.ds(pl.multiple_of(u * T + (k * 4 + x) * H, H), H)
         obuf[at, :] = total.astype(BF)
-        for n in range(7):
-            send(obuf.at[at], obuf.at[at], "o", ors.at[u], (t, r, col_of[n + 1]))
+        for n in (2, 1, 3):
+            for core in range(2):
+                send(obuf.at[at], obuf.at[at], "o", ors.at[u], (t, r, x_of[n] * 2 + core))
+        send(obuf.at[at], obuf.at[at], "o", ors.at[u], at_core)
 
     tn = (((0,), (0,)), ((), ()))
 

time: 90.2 us -> 89.1 us (0.988)
  Pallas kernels: 89.5 us -> 88.4 us
    pallas_call x1, Pallas kernels: 86.6 us -> 85.5 us  [on_device(): pl.pallas_call(comm_kernel, name='exchange', out_shape=[pltpu.VMEM(s, BF)...]
where the time goes in v6:
time: 89.1 us
  Pallas kernels  88.4 us (99%)
    pallas_call x1, Pallas kernels, on_device(): pl.pallas_call(comm_kernel, name='exchange', out_shape=[pltpu.VMEM(s, BF)...  85.5 us
    pallas_call x1, Pallas kernels, on_device(): pl.pallas_call(store_kernel, name='store', out_shape=[jax.ShapeDtypeStruc...  2.9 us

profile of v6, /device:TPU:1, one launch (start us, length us, event | category | flops | bytes accessed | tf_op | source)
XLA Modules:
  0.0 89.1 jit_solution(14177191662756551270)
XLA Ops:
  0.6 85.5 %exchange.1 = (bf16[256,1024]{1,0:T(8,128)(2,1)S(1)}, bf16[1024,512]{1,0:T(8,128)(2,1)S(1)}, bf16[1024,512]{1,0:T(8,128)(2,1)S(1)}, bf16[512,1024]{1,0:T(8,128)(...) custom-call(bf16[256,1024]{1,0:T(8,128)(2,1)} %tokens.1, ...), custom_call_target="tpu_custom_call" | custom-call | tf_op jit(solution)/shard_map/exchange/pallas_call | solution.py:392
  86.2 2.9 %store.1 = (bf16[256,1024]{1,0:T(8,128)(2,1)}, bf16[1024,512]{1,0:T(8,128)(2,1)}, bf16[1024,512]{1,0:T(8,128)(2,1)}, bf16[512,1024]{1,0:T(8,128)(2,1)}, bf16[102...) custom-call(bf16[256,1024]{1,0:T(8,128)(2,1)S(1)} %get-tuple-element.14.refs_0_, ...), custom_call_target="tpu_custom_call" | custom-call | tf_op jit(solution)/shard_map/store/pallas_call | solution.py:453

commit v7 on v6

--- a/solution.py
+++ b/solution.py
@@ -339,11 +339,11 @@
     loads[0].wait()
     loads[1].wait()
     prepare(0)
+    prepare(1)
     pl.semaphore_wait(barrier, len(peers))
     for i in range(NCH):
         if BLOCK[i] and ("az", i) not in ORDER:
             stage_az(i)
-    prepare(1)
     prepare(2)
     stages = dict(
         az=stage_az, ax=stage_ax, ac=stage_ac, s1=stage_s1, s2=stage_s2, s3=stage_s3, s4=stage_s4,

time: 89.1 us -> 90.1 us (1.011)
  Pallas kernels: 88.4 us -> 89.4 us
    pallas_call x1, Pallas kernels: 85.5 us -> 86.5 us  [on_device(): pl.pallas_call(comm_kernel, name='exchange', out_shape=[pltpu.VMEM(s, BF)...]
where the time goes in v7:
time: 90.1 us; the launch traced here: 90 us
  Pallas kernels  89.4 us (99%)
    pallas_call x1, Pallas kernels, on_device(): pl.pallas_call(comm_kernel, name='exchange', out_shape=[pltpu.VMEM(s, BF)...  86.5 us
    pallas_call x1, Pallas kernels, on_device(): pl.pallas_call(store_kernel, name='store', out_shape=[jax.ShapeDtypeStruc...  2.9 us

profile of v7, /device:TPU:1, one launch (start us, length us, event | category | flops | bytes accessed | tf_op | source)
XLA Modules:
  0.0 90.0 jit_solution(2542348504410910173)
XLA Ops:
  0.6 86.5 %exchange.1 = (bf16[256,1024]{1,0:T(8,128)(2,1)S(1)}, bf16[1024,512]{1,0:T(8,128)(2,1)S(1)}, bf16[1024,512]{1,0:T(8,128)(2,1)S(1)}, bf16[512,1024]{1,0:T(8,128)(...) custom-call(bf16[256,1024]{1,0:T(8,128)(2,1)} %tokens.1, ...), custom_call_target="tpu_custom_call" | custom-call | tf_op jit(solution)/shard_map/exchange/pallas_call | solution.py:392
  87.1 2.9 %store.1 = (bf16[256,1024]{1,0:T(8,128)(2,1)}, bf16[1024,512]{1,0:T(8,128)(2,1)}, bf16[1024,512]{1,0:T(8,128)(2,1)}, bf16[512,1024]{1,0:T(8,128)(2,1)}, bf16[102...) custom-call(bf16[256,1024]{1,0:T(8,128)(2,1)S(1)} %get-tuple-element.14.refs_0_, ...), custom_call_target="tpu_custom_call" | custom-call | tf_op jit(solution)/shard_map/store/pallas_call | solution.py:453
